TPU v7x, 32 devices: a whole 2x2x4 slice. The times are simulated.
32 devices in a mesh: groups: 2 (over x), table: 16 (over z, y, core).
Axes of the slice: x: 2, y: 2, z: 4, core: 2. Of those that a mesh axis runs over, the one named last changes fastest.
Arguments:
- hidden: bfloat16 [8192, 2560], P(('groups', 'table')), parts along dimension 0, may hold values from -6 to 6
- cotangent: bfloat16 [8192, 2560], P(('groups', 'table')), parts along dimension 0, may hold values from -6 to 6
- row_owner: int32 [8192, 8], P(('groups', 'table')), parts along dimension 0, may hold values from 0 to 15, all different within a row; in each aligned block of 256 rows (0 to 255, 256 to 511, ...) at most 256 rows name the same one
- row_slot: int32 [8192, 8], P(('groups', 'table')), parts along dimension 0, may hold values from 0 to 9215
- ngram_table: bfloat16 [147456, 160], P('table'), may hold values from -6 to 6
- w_key: bfloat16 [1280, 2560], P('table'), may hold values from -0.15625 to 0.15625
- w_value: bfloat16 [1280, 2560], P('table'), may hold values from -0.15625 to 0.15625
- conv_weight: float32 [4, 2560], replicated, may hold values from -3 to 3
Outputs:
- layer_out: bfloat16 [8192, 2560], P(('groups', 'table')), parts along dimension 0
- hidden_grad: bfloat16 [8192, 2560], P(('groups', 'table')), parts along dimension 0
- table_grad: bfloat16 [294912, 160], P(('groups', 'table')), parts along dimension 0
There are 2 independent parts, one for each index of `groups`. A program takes and returns all parts, laid end to end along the dimension named above; an argument that names none is the same for every part. Nothing has to cross between parts.
Inputs may be any that keep to these rules, and one draw needn't show every extreme that they name: `row_owner`: owner devices of a token's 8 heads differ; among the rows of one device no owner is named more than 256 times, and in some devices one owner is named exactly 256 times.
All inputs are finite; a program needn't handle non-finite values.
Results may differ from a plain program's by a relative error of at most 0.0054.
Values may be sent and summed in bfloat16 or wider, within the bound.
A program may use at most 128 MiB of HBM per device.

v0:
```python
import math

import jax
import jax.numpy as jnp
from jax import lax
from jax.sharding import PartitionSpec as P

LENGTH = 4096
MAX_GRAM_ORDER = 3


epsilon = 1e-06


def shifted(value, axis, by):
    peers = lax.axis_size(axis)
    pairs = [(i, i + by) for i in range(peers) if 0 <= i + by < peers]
    return lax.ppermute(value, axis, pairs)


def inverse_rms(values):
    return lax.rsqrt(jnp.mean(values * values, axis=-1, keepdims=True) + epsilon)


def contract_last(left, right):
    return lax.dot_general(
        left, right, (((1,), (1,)), ((), ())), preferred_element_type=jnp.float32
    )


def on_device(hidden, cotangent, row_owner, row_slot, ngram_table, w_key, w_value, conv_weight):
    tokens_here, heads = row_owner.shape
    row_width = ngram_table.shape[1]
    width = hidden.shape[1]
    devices = lax.axis_size("table")
    entries = tokens_here * heads
    capacity = 2 * entries // devices
    flat_owner = row_owner.reshape(-1)
    one_hot = (flat_owner[:, None] == jnp.arange(devices, dtype=jnp.int32)[None, :]).astype(
        jnp.int32
    )
    earlier = jnp.cumsum(one_hot, axis=0) - one_hot
    rank = jnp.sum(earlier * one_hot, axis=1)
    place = flat_owner * capacity + rank
    requests = (
        jnp.zeros((devices * capacity,), jnp.int32)
        .at[place]
        .set(row_slot.reshape(-1))
        .reshape(devices, capacity)
    )
    wanted_row_list = lax.all_to_all(requests, "table", split_axis=0, concat_axis=0, tiled=True)
    replies = lax.all_to_all(
        ngram_table[wanted_row_list], "table", split_axis=0, concat_axis=0, tiled=True
    )
    memory = replies.reshape(devices * capacity, row_width)[place].reshape(
        tokens_here, heads * row_width
    )
    stacked = jnp.stack((w_key, w_value))
    whole = lax.all_gather(stacked, "table", axis=1, tiled=True)
    keys_proj = jnp.dot(memory, whole[0], preferred_element_type=jnp.float32)
    values_proj = jnp.dot(memory, whole[1], preferred_element_type=jnp.float32)
    hidden_f = hidden.astype(jnp.float32)
    hidden_scale_factor = inverse_rms(hidden_f)
    scale_keys = inverse_rms(keys_proj)
    hidden_n = hidden_f * hidden_scale_factor
    keys_n = keys_proj * scale_keys
    root_width = math.sqrt(width)
    score = jnp.sum(hidden_n * keys_n, axis=-1, keepdims=True) / root_width
    gate = jax.nn.sigmoid(score)
    gated = gate * values_proj
    scale_gated = inverse_rms(gated)
    normed = (gated * scale_gated).astype(jnp.bfloat16)
    kernel_taps = conv_weight.shape[0]
    border_rows = (kernel_taps - 1) * MAX_GRAM_ORDER
    window = LENGTH
    position = (
        lax.axis_index("table") * tokens_here + jnp.arange(tokens_here, dtype=jnp.int32)
    ) % window
    before_rows = shifted(normed[tokens_here - border_rows :], "table", 1)
    extended = jnp.concatenate([before_rows, normed], axis=0)
    mixed = jnp.zeros((tokens_here, width), jnp.float32)
    for kernel_tap_index in range(kernel_taps):
        start_offset = kernel_tap_index * MAX_GRAM_ORDER
        moved = extended[
            border_rows - start_offset : border_rows - start_offset + tokens_here
        ].astype(jnp.float32)
        mixed = mixed + conv_weight[kernel_tap_index] * jnp.where(
            (position >= start_offset)[:, None], moved, 0.0
        )
    layer_out = (jax.nn.silu(mixed) + gated).astype(jnp.bfloat16)
    upstream = cotangent.astype(jnp.float32)
    sigm = jax.nn.sigmoid(mixed)
    slope = upstream * sigm * (1.0 + mixed * (1.0 - sigm))
    after_rows = shifted(slope[:border_rows], "table", -1)
    following = jnp.concatenate([slope, after_rows], axis=0)
    normed_grad = jnp.zeros((tokens_here, width), jnp.float32)
    for kernel_tap_index in range(kernel_taps):
        start_offset = kernel_tap_index * MAX_GRAM_ORDER
        moved = following[start_offset : start_offset + tokens_here]
        normed_grad = normed_grad + conv_weight[kernel_tap_index] * jnp.where(
            (position + start_offset < window)[:, None], moved, 0.0
        )
    gated_grad = (
        upstream
        + scale_gated * normed_grad
        - scale_gated**3 * gated * jnp.sum(normed_grad * gated, axis=-1, keepdims=True) / width
    )
    values_grad = (gate * gated_grad).astype(jnp.bfloat16)
    score_grad = jnp.sum(gated_grad * values_proj, axis=-1, keepdims=True) * gate * (1.0 - gate)
    keys_n_grad = score_grad * hidden_n / root_width
    hidden_n_grad = score_grad * keys_n / root_width
    keys_grad = (
        scale_keys * keys_n_grad
        - scale_keys**3
        * keys_proj
        * jnp.sum(keys_n_grad * keys_proj, axis=-1, keepdims=True)
        / width
    ).astype(jnp.bfloat16)
    hidden_grad = (
        hidden_scale_factor * hidden_n_grad
        - hidden_scale_factor**3
        * hidden_f
        * jnp.sum(hidden_n_grad * hidden_f, axis=-1, keepdims=True)
        / width
    ).astype(jnp.bfloat16)
    memory_grad = contract_last(keys_grad, whole[0]) + contract_last(values_grad, whole[1])
    memory_grad = memory_grad.astype(jnp.bfloat16)
    outgoing = (
        jnp.zeros((devices * capacity, row_width), jnp.bfloat16)
        .at[place]
        .set(memory_grad.reshape(-1, row_width))
    )
    arrived = lax.all_to_all(
        outgoing.reshape(devices, capacity, row_width),
        "table",
        split_axis=0,
        concat_axis=0,
        tiled=True,
    )
    table_sum = (
        jnp.zeros(ngram_table.shape, jnp.float32)
        .at[wanted_row_list.reshape(-1)]
        .add(arrived.reshape(-1, row_width).astype(jnp.float32))
    )
    return (layer_out, hidden_grad, table_sum.astype(jnp.bfloat16))


def solution(mesh):
    in_specs = (
        P(("groups", "table"), None),
        P(("groups", "table"), None),
        P(("groups", "table"), None),
        P(("groups", "table"), None),
        P("table", None),
        P("table", None),
        P("table", None),
        P(),
    )
    out_specs = (
        P(("groups", "table"), None),
        P(("groups", "table"), None),
        P(("groups", "table"), None),
    )
    return jax.shard_map(
        on_device, mesh=mesh, in_specs=in_specs, out_specs=out_specs, check_vma=False
    )
```

profile of v0, /device:TPU:9, one launch (start us, length us, event | category | flops | bytes accessed | tf_op | source)
XLA Modules:
  0.0 292.4 jit_solution(17860637846863159638)
XLA Ops:
  7.2 2.2 pad_maximum_fusion.2
  9.5 0.8 copy.28
  10.6 0.1 copy.27
  10.7 0.1 mul.273
  10.9 4.5 %reduce-window.6 = s32[16,16,128]{2,1,0:T(8,128)S(1)} reduce-window(s32[16,16,128]{2,1,0:T(8,128)S(1)} %fusion.51, s32[]{:T(128)} %constant.24.clone.1), window={size=1x1x128 pad=0_0x0_0x127_0}, to_apply=%region_1.2 | reduce-window | flops 4161536 | bytes 262148 | tf_op jit(solution)/shard_map/reduce-window
  15.4 0.4 slice_reduce_fusion
  15.8 0.2 reduce-window.9
  16.0 0.1 copy.30
  16.1 0.1 reshape.269
  16.5 8.6 %scatter_custom_fusion = s32[4096]{0:T(1024)} fusion(s32[2048]{0:T(1024)S(1)} %bitcast.62, s32[2048]{0:T(1024)S(1)} %reshape.269, s32[]{:T(128)} %constant.24.clone.1), kind=kCustom, calls=%fused_computation.95 | custom fusion | bytes 16388 | tf_op jit(solution)/shard_map/scatter | solution.py:48
  25.1 6.6 %all-to-all-start = ((s32[16,1,256]{2,1,0:T(1,128)}), s32[16,1,256]{2,1,0:T(1,128)S(1)}, u32[]{:S(2)}, u32[]{:S(2)}) async-start(s32[16,1,256]{2,1,0:T(1,128)} %bitcast.3), calls=%async_computation | async-start | bytes 32768 | tf_op jit(solution)/shard_map/all_to_all | solution.py:51
  31.7 4.0 %copy.31 = bf16[9216,160]{1,0:T(8,128)(2,1)} copy(bf16[9216,160]{0,1:T(8,128)(2,1)S(1)} %copy-done.3) | data formatting | bytes 5898240 | tf_op args[4]
  35.7 1.0 all-to-all-done
  36.7 16.0 %gather_fusion = bf16[4096,160]{1,0:T(8,128)(2,1)S(1)} fusion(bf16[9216,160]{1,0:T(8,128)(2,1)} %copy.31, s32[4096]{0:T(1024)S(1)} %broadcast_clamp_fusion), kind=kCustom, calls=%fused_computation | custom fusion | bytes 2637824 | tf_op jit(solution)/shard_map/gather | solution.py:53
  52.7 2.2 copy.32
  54.9 5.3 %all-to-all-start.1 = ((bf16[16,256,160]{1,2,0:T(8,128)(2,1)}), bf16[16,256,160]{1,2,0:T(8,128)(2,1)S(1)}, u32[]{:S(2)}, u32[]{:S(2)}) async-start(bf16[16,256,160]{1,2,0:T(8,128)(2,1)} %copy.32), calls=%async_computation.1 | async-start | bytes 2621440 | tf_op jit(solution)/shard_map/all_to_all | solution.py:52
  60.4 0.3 fusion.27
  60.8 63.9 %all-to-all-done.1 = bf16[16,256,160]{1,2,0:T(8,128)(2,1)S(1)} async-done(((bf16[16,256,160]{1,2,0:T(8,128)(2,1)}), bf16[16,256,160]{1,2,0:T(8,128)(2,1)S(1)}, u32[]{:S(2)}, u32[]{:S(2)}) %all-to-all-start.1) | async-done | bytes 1310752 | tf_op jit(solution)/shard_map/all_to_all | solution.py:52
  124.7 1.8 copy.33
  126.5 7.5 %gather_fusion.1 = bf16[2048,160]{1,0:T(8,128)(2,1)S(1)} fusion(bf16[4096,160]{1,0:T(8,128)(2,1)S(1)} %bitcast.52, s32[2048]{0:T(1024)S(1)} %broadcast_clamp_fusion.1), kind=kCustom, calls=%fused_computation.1 | custom fusion | bytes 1318912 | tf_op jit(solution)/shard_map/gather | solution.py:55
  134.0 2.0 reshape.244
  136.0 0.9 all-gather.2.cloned.1.call-done
  137.0 5.1 %multiply_reduce_fusion.3 = (f32[256]{0:T(256)S(1)}, f32[256,2560]{1,0:T(8,128)S(1)}) fusion(bf16[256,1280]{1,0:T(8,128)(2,1)} %reshape.244, bf16[2,1280,2560]{2,1,0:T(8,128)(2,1)} %all-gather.2.cloned.1.call-done), kind=kOutput, calls=%fused_computation.61 | convolution fusion | flops 1679032064 | bytes 9831424 | tf_op jit(solution)/shard_map/dot_general | solution.py:60
  142.1 0.6 fusion.24
  142.7 1.4 copy-done.8
  144.1 0.3 copy-done.4
  144.4 1.9 multiply_reduce_fusion.2
  146.4 0.3 multiply_convert_fusion.1
  146.8 4.9 %collective-permute-start = (bf16[9,2560]{1,0:T(8,128)(2,1)S(1)}, bf16[9,2560]{1,0:T(8,128)(2,1)S(1)}, u32[]{:S(2)}, u32[]{:S(2)}) collective-permute-start(bf16[9,2560]{1,0:T(8,128)(2,1)S(1)} %slice.78), channel_id=1, source_target_pairs={{0,1},{1,2},{2,3},{3,4},{4,5},{5,6},{6,7},{7,8},{8,9},{9,10},{10,1... | collective-permute-start | bytes 138248 | tf_op jit(solution)/shard_map/ppermute | solution.py:18
  151.7 1.3 collective-permute-done
  153.0 3.4 %fusion.25 = (f32[256,2560]{1,0:T(8,128)S(1)}, f32[256,2560]{1,0:T(8,128)S(1)}) fusion(bf16[256,2560]{1,0:T(8,128)(2,1)S(1)} %copy-done.2, bf16[256,2560]{1,0:T(8,128)(2,1)S(1)} %multiply_convert_fusion.1, bf16[9,2560]{1,0:T(8,128)(2,1)S(1)} %collective-permute-done, pred[256]{0:T(512)(128)(4,1)S(1)} %get-tuple-element.40, f32[2560]{0:T(1024)S(1)} %get-tuple-element.16, ...), kind=kLoop, calls=%fused_computation.42 | loop fusion | flops 21626880 | bytes 7952384 | tf_op jit(solution)/shard_map/mul | solution.py:93
  156.4 6.7 %collective-permute-start.1 = (f32[9,2560]{1,0:T(8,128)S(1)}, f32[9,2560]{1,0:T(8,128)S(1)}, u32[]{:S(2)}, u32[]{:S(2)}) collective-permute-start(f32[9,2560]{1,0:T(8,128)S(1)} %slice.83), channel_id=1, source_target_pairs={{1,0},{2,1},{3,2},{4,3},{5,4},{6,5},{7,6},{8,7},{9,8},{10,9},{11,1... | collective-permute-start | bytes 276488 | tf_op jit(solution)/shard_map/ppermute | solution.py:18
  163.2 1.0 collective-permute-done.1
  164.2 4.0 %multiply_reduce_fusion.1 = (f32[256]{0:T(256)S(1)}, f32[256,2560]{1,0:T(8,128)S(1)}) fusion(f32[256,2560]{1,0:T(8,128)S(1)} %get-tuple-element.35, f32[256]{0:T(256)S(1)} %add_divide_fusion.1, f32[9,2560]{1,0:T(8,128)S(1)} %collective-permute-done.1, f32[256,2560]{1,0:T(8,128)S(1)} %get-tuple-element.20, pred[256]{0:T(512)(128)(4,1)S(1)} %get-tuple-element.36, ...), kind=kLoop, calls=%fused_computation.55 | loop fusion | flops 11140864 | bytes 8000512 | tf_op jit(solution)/shard_map/reduce_sum | solution.py:106
  168.2 2.5 multiply_reduce_fusion
  170.7 1.5 fusion.23
  172.2 5.2 %fusion = f32[256,1280]{1,0:T(8,128)S(1)} fusion(bf16[2,1280,2560]{2,1,0:T(8,128)(2,1)} %all-gather.2.cloned.1.call-done, bf16[256,2560]{1,0:T(8,128)(2,1)S(1)} %copy-done.1, f32[256,2560]{1,0:T(8,128)S(1)} %get-tuple-element.33, f32[256]{0:T(256)S(1)} %get-tuple-element.12, f32[256]{0:T(256)S(1)} %get-tuple-element.25, f32[256]{0:T(256)S(1)} %get-tuple-element.24, ...), kind=kOutput, calls=%fused_computation.7 | convolution fusion | flops 1683619840 | bytes 11801600 | tf_op jit(solution)/shard_map/dot_general | solution.py:26
  177.4 5.2 %fusion.35 = bf16[256,1280]{1,0:T(8,128)(2,1)S(1)} fusion(f32[256,1280]{1,0:T(8,128)S(1)} %fusion, bf16[2,1280,2560]{2,1,0:T(8,128)(2,1)} %all-gather.2.cloned.1.call-done, f32[256]{0:T(256)S(1)} %add_divide_fusion.1, bf16[256,2560]{1,0:T(8,128)(2,1)S(1)} %copy-done.2, f32[256,2560]{1,0:T(8,128)S(1)} %get-tuple-element.19, ...), kind=kOutput, calls=%fused_computation.62 | convolution fusion | flops 1684930560 | bytes 15077376 | tf_op jit(solution)/shard_map/dot_general | solution.py:26
  182.7 2.3 reshape.277
  185.0 11.5 %scatter_custom_fusion.1 = bf16[4096,160]{1,0:T(8,128)(2,1)} fusion(s32[2048]{0:T(1024)S(1)} %bitcast.64, bf16[2048,160]{1,0:T(8,128)(2,1)} %reshape.277, bf16[]{:T(256)} %constant.68.clone.1), kind=kCustom, calls=%fused_computation.75 | custom fusion | bytes 1311232 | tf_op jit(solution)/shard_map/scatter | solution.py:131
  196.4 3.7 %copy.34 = bf16[16,256,160]{1,2,0:T(8,128)(2,1)} copy(bf16[16,256,160]{2,1,0:T(8,128)(2,1)} %bitcast.53) | data formatting | bytes 2621440 | tf_op jit(solution)/shard_map/reshape | solution.py:134
  200.2 7.2 %all-to-all-start.2 = ((bf16[16,256,160]{1,2,0:T(8,128)(2,1)}), bf16[16,256,160]{1,2,0:T(8,128)(2,1)}, u32[]{:S(2)}, u32[]{:S(2)}) async-start(bf16[16,256,160]{1,2,0:T(8,128)(2,1)} %copy.34), calls=%async_computation.2 | async-start | bytes 2621440 | tf_op jit(solution)/shard_map/all_to_all | solution.py:133
  207.4 3.3 %fusion.31 = bf16[256,2560]{1,0:T(8,128)(2,1)} fusion(bf16[256,2560]{1,0:T(8,128)(2,1)} %param.8, f32[256,2560]{1,0:T(8,128)S(1)} %get-tuple-element.33, f32[256]{0:T(256)S(1)} %get-tuple-element.13, f32[256]{0:T(256)S(1)} %get-tuple-element.28, f32[256]{0:T(256)S(1)} %get-tuple-element.27, f32[256]{0:T(256)S(1)} %subtract_multiply_fusion, ...), kind=kLoop, calls=%fused_computation.48 | loop fusion | flops 5898240 | bytes 5248000 | tf_op jit(solution)/shard_map/convert_element_type | solution.py:125
  210.6 27.0 %all-to-all-done.2 = bf16[16,256,160]{1,2,0:T(8,128)(2,1)} async-done(((bf16[16,256,160]{1,2,0:T(8,128)(2,1)}), bf16[16,256,160]{1,2,0:T(8,128)(2,1)}, u32[]{:S(2)}, u32[]{:S(2)}) %all-to-all-start.2) | async-done | bytes 1310752 | tf_op jit(solution)/shard_map/all_to_all | solution.py:133
  237.6 3.8 %copy.38 = f32[16,256,160]{2,1,0:T(8,128)} copy(bf16[16,256,160]{1,2,0:T(8,128)(2,1)} %all-to-all-done.2) | data formatting | bytes 3932160 | tf_op jit(solution)/shard_map/convert_element_type | solution.py:143
  241.5 32.0 %scatter_custom_fusion.2 = f32[9216,160]{1,0:T(8,128)} fusion(s32[4096]{0:T(1024)S(1)} %bitcast.66, f32[4096,160]{1,0:T(8,128)} %bitcast.55, f32[]{:T(128)} %constant.29.clone.1), kind=kCustom, calls=%fused_computation.11 | custom fusion | flops 655360 | bytes 5898752 | tf_op jit(solution)/shard_map/scatter-add | solution.py:143
  273.5 6.0 %convert_element_type.68 = bf16[9216,160]{1,0:T(8,128)(2,1)} convert(f32[9216,160]{1,0:T(8,128)} %scatter_custom_fusion.2) | non-fusion elementwise | flops 1474560 | bytes 8847360 | tf_op jit(solution)/shard_map/convert_element_type | solution.py:145
  279.5 6.1 %copy.37 = bf16[9216,160]{0,1:T(8,128)(2,1)} copy(bf16[9216,160]{1,0:T(8,128)(2,1)} %convert_element_type.68) | data formatting | bytes 5898240
  (41 shorter events, 0.8 us)
Async XLA Ops:
  7.2 3.4 %copy-start.6 = (s32[256,8]{0,1:T(8,128)S(1)}, s32[256,8]{0,1:T(8,128)}, u32[]{:S(2)}) copy-start(s32[256,8]{0,1:T(8,128)} %param.10) | copy-start | bytes 24580
  7.2 8.8 %copy-start.7 = (s32[256,8]{0,1:T(8,128)S(1)}, s32[256,8]{0,1:T(8,128)}, u32[]{:S(2)}) copy-start(s32[256,8]{0,1:T(8,128)} %param.11) | copy-start | bytes 24580
  7.2 24.5 %copy-start.3 = (bf16[9216,160]{0,1:T(8,128)(2,1)S(1)}, bf16[9216,160]{0,1:T(8,128)(2,1)}, u32[]{:S(2)}) copy-start(bf16[9216,160]{0,1:T(8,128)(2,1)} %param.12) | copy-start | bytes 8847364
  7.2 129.8 %all-gather.2.cloned.1.call-start = ((), (), s32[]{:S(2)}) async-start(), calls=%async_computation.3 | async-start | bytes 13926400 | tf_op jit(solution)/shard_map/all_gather | solution.py:59
  25.1 11.6 %all-to-all-start = ((s32[16,1,256]{2,1,0:T(1,128)}), s32[16,1,256]{2,1,0:T(1,128)S(1)}, u32[]{:S(2)}, u32[]{:S(2)}) async-start(s32[16,1,256]{2,1,0:T(1,128)} %bitcast.3), calls=%async_computation | async-start | bytes 32768 | tf_op jit(solution)/shard_map/all_to_all | solution.py:51
  52.7 7.6 %copy-start.5 = (f32[4,2560]{1,0:T(4,128)S(1)}, f32[4,2560]{1,0:T(4,128)}, u32[]{:S(2)}) copy-start(f32[4,2560]{1,0:T(4,128)} %param.15) | copy-start | bytes 122884
  52.7 7.7 %copy-start = (bf16[256,2560]{1,0:T(8,128)(2,1)S(1)}, bf16[256,2560]{1,0:T(8,128)(2,1)}, u32[]{:S(2)}) copy-start(bf16[256,2560]{1,0:T(8,128)(2,1)} %param.8) | copy-start | bytes 3932164
  54.9 69.8 %all-to-all-start.1 = ((bf16[16,256,160]{1,2,0:T(8,128)(2,1)}), bf16[16,256,160]{1,2,0:T(8,128)(2,1)S(1)}, u32[]{:S(2)}, u32[]{:S(2)}) async-start(bf16[16,256,160]{1,2,0:T(8,128)(2,1)} %copy.32), calls=%async_computation.1 | async-start | bytes 2621440 | tf_op jit(solution)/shard_map/all_to_all | solution.py:52
  137.0 5.2 %copy-start.1 = (bf16[256,2560]{1,0:T(8,128)(2,1)S(1)}, bf16[256,2560]{1,0:T(8,128)(2,1)}, u32[]{:S(2)}) copy-start(bf16[256,2560]{1,0:T(8,128)(2,1)} %param.8) | copy-start | bytes 3932164
  137.0 7.2 %copy-start.8 = (bf16[2,1280,2560]{2,1,0:T(8,128)(2,1)S(1)}, bf16[2,1280,2560]{2,1,0:T(8,128)(2,1)}, u32[]{:S(2)}) copy-start(bf16[2,1280,2560]{2,1,0:T(8,128)(2,1)} %all-gather.2.cloned.1.call-done) | copy-start | bytes 39321604
  142.1 2.3 copy-start.4
  146.4 6.6 %copy-start.2 = (bf16[256,2560]{1,0:T(8,128)(2,1)S(1)}, bf16[256,2560]{1,0:T(8,128)(2,1)}, u32[]{:S(2)}) copy-start(bf16[256,2560]{1,0:T(8,128)(2,1)} %param.9) | copy-start | bytes 3932164
  146.8 6.2 %collective-permute-start = (bf16[9,2560]{1,0:T(8,128)(2,1)S(1)}, bf16[9,2560]{1,0:T(8,128)(2,1)S(1)}, u32[]{:S(2)}, u32[]{:S(2)}) collective-permute-start(bf16[9,2560]{1,0:T(8,128)(2,1)S(1)} %slice.78), channel_id=1, source_target_pairs={{0,1},{1,2},{2,3},{3,4},{4,5},{5,6},{6,7},{7,8},{8,9},{9,10},{10,1... | collective-permute-start | bytes 138248 | tf_op jit(solution)/shard_map/ppermute | solution.py:18
  156.4 7.8 %collective-permute-start.1 = (f32[9,2560]{1,0:T(8,128)S(1)}, f32[9,2560]{1,0:T(8,128)S(1)}, u32[]{:S(2)}, u32[]{:S(2)}) collective-permute-start(f32[9,2560]{1,0:T(8,128)S(1)} %slice.83), channel_id=1, source_target_pairs={{1,0},{2,1},{3,2},{4,3},{5,4},{6,5},{7,6},{8,7},{9,8},{10,9},{11,1... | collective-permute-start | bytes 276488 | tf_op jit(solution)/shard_map/ppermute | solution.py:18
  200.2 37.5 %all-to-all-start.2 = ((bf16[16,256,160]{1,2,0:T(8,128)(2,1)}), bf16[16,256,160]{1,2,0:T(8,128)(2,1)}, u32[]{:S(2)}, u32[]{:S(2)}) async-start(bf16[16,256,160]{1,2,0:T(8,128)(2,1)} %copy.34), calls=%async_computation.2 | async-start | bytes 2621440 | tf_op jit(solution)/shard_map/all_to_all | solution.py:133
Sparse Core Ops, SparseCore 0:
  10.9 126.0 all-gather.1
where the time goes:
time: 293 us; the launch traced here: 292 us
  waiting for transfers between devices  95.1 us (32%)
  local copies, waits for them, and re-layouts  73.4 us (25%)
  other arithmetic  61.3 us (21%)
  starting transfers between devices  30.8 us (11%)
  matrix products  17.5 us (6%)
  between operations  14.4 us (5%)
    all_to_all x1, waiting for transfers between devices, on_device(): lax.all_to_all(ngram_table[wanted_row_list], 'table', split_axis=0, conca...  63.9 us
    scatter-add x1, other arithmetic, on_device(): table_sum = jnp.zeros(ngram_table.shape, jnp.float32).at[wanted_row_list....  32 us
    all_to_all x1, waiting for transfers between devices, on_device(): lax.all_to_all(outgoing.reshape(devices, capacity, row_width), 'table', s...  27 us
    gather x2, local copies, waits for them, and re-layouts, on_device(): ngram_table[wanted_row_list]  18.2 us
    unnamed x22, local copies, waits for them, and re-layouts  12.8 us
    ppermute x2, starting transfers between devices, shifted(): return lax.ppermute(value, axis, pairs)  11.7 us
    scatter x1, local copies, waits for them, and re-layouts, on_device(): outgoing = jnp.zeros((devices * capacity, row_width), jnp.bfloat16).at[pl...  11.5 us
    dot_general x2, matrix products, contract_last(): lax.dot_general(left, right, (((1,), (1,)), ((), ())), preferred_element_...  10.4 us
  transfers between devices with their start and end apart: 6, of which 6 were waited for; matrix products, arithmetic and copies ran while one was open for 18% of the time, Pallas kernels for 0%

commit v1 on v0

--- a/solution.py
+++ b/solution.py
@@ -1,8 +1,11 @@
+import functools
 import math
 
 import jax
 import jax.numpy as jnp
 from jax import lax
+from jax.experimental import pallas as pl
+from jax.experimental.pallas import tpu as pltpu
 from jax.sharding import PartitionSpec as P
 
 LENGTH = 4096
@@ -26,6 +29,268 @@
     return lax.dot_general(
         left, right, (((1,), (1,)), ((), ())), preferred_element_type=jnp.float32
     )
+
+
+def contract_first(left, right):
+    return lax.dot_general(
+        left, right, (((0,), (0,)), ((), ())), preferred_element_type=jnp.float32
+    )
+
+
+CHUNK = 1024
+MESH = pl.DeviceIdType.MESH
+
+
+def enter(group, me, devices):
+    barrier = pltpu.get_barrier_semaphore()
+
+    def greet(i, carry):
+        pl.semaphore_signal(
+            barrier, inc=1, device_id=(group, lax.rem(me + i, devices)), device_id_type=MESH
+        )
+        return carry
+
+    lax.fori_loop(1, devices, greet, 0)
+    pl.semaphore_wait(barrier, devices - 1)
+
+
+def picks(slots, start, rows):
+    tokens = slots.shape[1]
+    number = lax.broadcasted_iota(jnp.int32, (rows, tokens), 0) + start
+    return jnp.where(number == slots, 1.0, 0.0).astype(jnp.bfloat16)
+
+
+def chunks_of(rows):
+    return [(start, min(CHUNK, rows - start)) for start in range(0, rows, CHUNK)]
+
+
+def fetch_kernel(
+    devices, req, tab, wk, wv, weights, replies, wanted, out_rows,
+    ring_send, ring_recv, core_send, core_recv, req_send, req_recv, rep_send, rep_recv, own_sem,
+):
+    group, me = lax.axis_index("groups"), lax.axis_index("table")
+    chips = devices // 2
+    half_ring = chips // 2
+    core, chip = me % 2, me // 2
+    odd = chip % 2
+    pos = (1 - odd) * (chip // 2) + odd * (chips - 1 - chip // 2)
+
+    def at_ring(r):
+        r = (r + 2 * chips) % chips
+        late = r // half_ring
+        return ((1 - late) * (2 * r) + late * (2 * (chips - 1 - r) + 1)) * 2 + core
+
+    partner = me + 1 - 2 * core
+    ways = (at_ring(pos + 1), at_ring(pos - 1))
+    half = wk.shape[1] // 2
+    parts = (wk, wv)
+
+    def block(d, kv, origin):
+        return weights.at[kv, origin, :, pl.ds(d * half, half)]
+
+    def ring_copy(d, kv, s):
+        sign = 1 - 2 * d
+        origin = at_ring(pos - sign * s)
+        source = parts[kv].at[:, pl.ds(d * half, half)] if s == 0 else block(d, kv, origin)
+        return pltpu.make_async_remote_copy(
+            src_ref=source, dst_ref=block(d, kv, origin),
+            send_sem=ring_send.at[d, kv, s], recv_sem=ring_recv.at[d, kv, s],
+            device_id=(group, ways[d]), device_id_type=MESH,
+        )
+
+    def core_copy(d, kv, s):
+        sign = 1 - 2 * d
+        origin = at_ring(pos - sign * s)
+        source = parts[kv].at[:, pl.ds(d * half, half)] if s == 0 else block(d, kv, origin)
+        return pltpu.make_async_remote_copy(
+            src_ref=source, dst_ref=block(d, kv, origin),
+            send_sem=core_send.at[d, kv, s], recv_sem=core_recv.at[d, kv, s],
+            device_id=(group, partner), device_id_type=MESH,
+        )
+
+    def own_copy(kv):
+        return pltpu.make_async_copy(parts[kv], weights.at[kv, me], own_sem.at[kv])
+
+    def req_copy(i):
+        to = lax.rem(me + i, devices)
+        return pltpu.make_async_remote_copy(
+            src_ref=req.at[to], dst_ref=wanted.at[me],
+            send_sem=req_send.at[i], recv_sem=req_recv.at[i],
+            device_id=(group, to), device_id_type=MESH,
+        )
+
+    def rep_copy(i):
+        to = lax.rem(me - i + devices, devices)
+        return pltpu.make_async_remote_copy(
+            src_ref=out_rows.at[to], dst_ref=replies.at[me],
+            send_sem=rep_send.at[i], recv_sem=rep_recv.at[i],
+            device_id=(group, to), device_id_type=MESH,
+        )
+
+    enter(group, me, devices)
+
+    def send_request(i, carry):
+        req_copy(i).start()
+        return carry
+
+    lax.fori_loop(1, devices, send_request, 0)
+    for kv in range(2):
+        for d in range(2):
+            ring_copy(d, kv, 0).start()
+    for kv in range(2):
+        own_copy(kv).start()
+        for d in range(2):
+            core_copy(d, kv, 0).start()
+
+    def pass_on(s):
+        for kv in range(2):
+            for d in range(2):
+                ring_copy(d, kv, s).wait_recv()
+                if s < chips - 2:
+                    ring_copy(d, kv, s + 1).start()
+                core_copy(d, kv, s + 1).start()
+
+    def look_up(slots):
+        total = None
+        for start, rows in chunks_of(tab.shape[1]):
+            term = jnp.dot(
+                tab[:, start : start + rows], picks(slots, start, rows),
+                preferred_element_type=jnp.float32,
+            )
+            total = term if total is None else total + term
+        return total.astype(jnp.bfloat16)
+
+    def answer(i, carry):
+        req_copy(i).wait_recv()
+        source = lax.rem(me - i + devices, devices)
+        out_rows[source] = look_up(wanted[source])
+        rep_copy(i).start()
+        return carry
+
+    first, second = devices * 3 // 8, devices * 3 // 4
+    lax.fori_loop(1, first, answer, 0)
+    pass_on(0)
+    lax.fori_loop(first, second, answer, 0)
+    pass_on(1)
+    lax.fori_loop(second, devices, answer, 0)
+    wanted[me] = req[me]
+    replies[me] = look_up(req[me])
+    for s in range(2, chips - 1):
+        pass_on(s)
+
+    def finish(i, carry):
+        req_copy(i).wait_send()
+        rep_copy(i).wait_send()
+        rep_copy(i).wait_recv()
+        return carry
+
+    lax.fori_loop(1, devices, finish, 0)
+    for kv in range(2):
+        own_copy(kv).wait()
+        for d in range(2):
+            for s in range(chips):
+                if s < chips - 1:
+                    ring_copy(d, kv, s).wait_send()
+                core_copy(d, kv, s).wait_send()
+                core_copy(d, kv, s).wait_recv()
+
+
+def fetch(requests, table_t, w_key, w_value):
+    devices, _, tokens = requests.shape
+    row_width = table_t.shape[0]
+    chips = devices // 2
+    vmem = pl.BlockSpec(memory_space=pltpu.VMEM)
+    hbm = pl.BlockSpec(memory_space=pl.ANY)
+    dma = pltpu.SemaphoreType.DMA
+    return pl.pallas_call(
+        functools.partial(fetch_kernel, devices),
+        out_shape=(
+            jax.ShapeDtypeStruct((2, devices) + w_key.shape, jnp.bfloat16),
+            jax.ShapeDtypeStruct((devices, row_width, tokens), jnp.bfloat16),
+            jax.ShapeDtypeStruct((devices, 1, tokens), jnp.int32),
+        ),
+        in_specs=[vmem, vmem, hbm, hbm],
+        out_specs=(hbm, vmem, vmem),
+        scratch_shapes=[
+            pltpu.VMEM((devices, row_width, tokens), jnp.bfloat16),
+            dma((2, 2, chips)), dma((2, 2, chips)), dma((2, 2, chips)), dma((2, 2, chips)),
+            dma((devices,)), dma((devices,)), dma((devices,)), dma((devices,)), dma((2,)),
+        ],
+        compiler_params=pltpu.CompilerParams(
+            collective_id=0, has_side_effects=True, vmem_limit_bytes=48 * 1024 * 1024
+        ),
+        name="fetch",
+    )(requests, table_t, w_key, w_value)
+
+
+def return_kernel(devices, out_grads, wanted, result, total, arrived, send, recv):
+    group, me = lax.axis_index("groups"), lax.axis_index("table")
+
+    def grad_copy(i):
+        to = lax.rem(me + i, devices)
+        return pltpu.make_async_remote_copy(
+            src_ref=out_grads.at[to], dst_ref=arrived.at[me],
+            send_sem=send.at[i], recv_sem=recv.at[i],
+            device_id=(group, to), device_id_type=MESH,
+        )
+
+    enter(group, me, devices)
+
+    def send_one(i, carry):
+        grad_copy(i).start()
+        return carry
+
+    lax.fori_loop(1, devices, send_one, 0)
+
+    def add(grads, slots, first):
+        for start, rows in chunks_of(total.shape[1]):
+            term = lax.dot_general(
+                grads, picks(slots, start, rows), (((1,), (1,)), ((), ())),
+                preferred_element_type=jnp.float32,
+            )
+            if first:
+                total[:, start : start + rows] = term
+            else:
+                total[:, start : start + rows] += term
+
+    add(out_grads[me], wanted[me], True)
+
+    def take(i, carry):
+        grad_copy(i).wait_recv()
+        source = lax.rem(me - i + devices, devices)
+        add(arrived[source], wanted[source], False)
+        return carry
+
+    lax.fori_loop(1, devices, take, 0)
+    for start, rows in chunks_of(total.shape[1]):
+        result[:, start : start + rows] = total[:, start : start + rows].astype(jnp.bfloat16)
+
+    def finish(i, carry):
+        grad_copy(i).wait_send()
+        return carry
+
+    lax.fori_loop(1, devices, finish, 0)
+
+
+def return_grads(out_grads, wanted, rows):
+    devices, row_width, tokens = out_grads.shape
+    vmem = pl.BlockSpec(memory_space=pltpu.VMEM)
+    dma = pltpu.SemaphoreType.DMA
+    return pl.pallas_call(
+        functools.partial(return_kernel, devices),
+        out_shape=jax.ShapeDtypeStruct((row_width, rows), jnp.bfloat16),
+        in_specs=[vmem, vmem],
+        out_specs=vmem,
+        scratch_shapes=[
+            pltpu.VMEM((row_width, rows), jnp.float32),
+            pltpu.VMEM((devices, row_width, tokens), jnp.bfloat16),
+            dma((devices,)), dma((devices,)),
+        ],
+        compiler_params=pltpu.CompilerParams(
+            collective_id=1, has_side_effects=True, vmem_limit_bytes=48 * 1024 * 1024
+        ),
+        name="return_grads",
+    )(out_grads, wanted)
 
 
 def on_device(hidden, cotangent, row_owner, row_slot, ngram_table, w_key, w_value, conv_weight):
@@ -33,32 +298,17 @@
     row_width = ngram_table.shape[1]
     width = hidden.shape[1]
     devices = lax.axis_size("table")
-    entries = tokens_here * heads
-    capacity = 2 * entries // devices
-    flat_owner = row_owner.reshape(-1)
-    one_hot = (flat_owner[:, None] == jnp.arange(devices, dtype=jnp.int32)[None, :]).astype(
-        jnp.int32
-    )
-    earlier = jnp.cumsum(one_hot, axis=0) - one_hot
-    rank = jnp.sum(earlier * one_hot, axis=1)
-    place = flat_owner * capacity + rank
-    requests = (
-        jnp.zeros((devices * capacity,), jnp.int32)
-        .at[place]
-        .set(row_slot.reshape(-1))
-        .reshape(devices, capacity)
-    )
-    wanted_row_list = lax.all_to_all(requests, "table", split_axis=0, concat_axis=0, tiled=True)
-    replies = lax.all_to_all(
-        ngram_table[wanted_row_list], "table", split_axis=0, concat_axis=0, tiled=True
-    )
-    memory = replies.reshape(devices * capacity, row_width)[place].reshape(
-        tokens_here, heads * row_width
-    )
-    stacked = jnp.stack((w_key, w_value))
-    whole = lax.all_gather(stacked, "table", axis=1, tiled=True)
-    keys_proj = jnp.dot(memory, whole[0], preferred_element_type=jnp.float32)
-    values_proj = jnp.dot(memory, whole[1], preferred_element_type=jnp.float32)
+    owner_t, slot_t = row_owner.T, row_slot.T
+    owners = jnp.arange(devices, dtype=jnp.int32)[:, None, None]
+    requests = jnp.max(jnp.where(owner_t[None] == owners, slot_t[None], -1), axis=1, keepdims=True)
+    gathered, replies, wanted_row_list = fetch(requests, ngram_table.T, w_key, w_value)
+    whole = gathered.reshape(2, -1, width)
+    memory_t = jnp.zeros((heads, row_width, tokens_here), jnp.bfloat16)
+    for owner in range(devices):
+        memory_t = jnp.where((owner_t == owner)[:, None, :], replies[owner][None], memory_t)
+    memory_t = memory_t.reshape(heads * row_width, tokens_here)
+    keys_proj = contract_first(memory_t, whole[0])
+    values_proj = contract_first(memory_t, whole[1])
     hidden_f = hidden.astype(jnp.float32)
     hidden_scale_factor = inverse_rms(hidden_f)
     scale_keys = inverse_rms(keys_proj)
@@ -123,26 +373,13 @@
         * jnp.sum(hidden_n_grad * hidden_f, axis=-1, keepdims=True)
         / width
     ).astype(jnp.bfloat16)
-    memory_grad = contract_last(keys_grad, whole[0]) + contract_last(values_grad, whole[1])
-    memory_grad = memory_grad.astype(jnp.bfloat16)
-    outgoing = (
-        jnp.zeros((devices * capacity, row_width), jnp.bfloat16)
-        .at[place]
-        .set(memory_grad.reshape(-1, row_width))
-    )
-    arrived = lax.all_to_all(
-        outgoing.reshape(devices, capacity, row_width),
-        "table",
-        split_axis=0,
-        concat_axis=0,
-        tiled=True,
-    )
-    table_sum = (
-        jnp.zeros(ngram_table.shape, jnp.float32)
-        .at[wanted_row_list.reshape(-1)]
-        .add(arrived.reshape(-1, row_width).astype(jnp.float32))
-    )
-    return (layer_out, hidden_grad, table_sum.astype(jnp.bfloat16))
+    memory_grad_t = contract_last(whole[0], keys_grad) + contract_last(whole[1], values_grad)
+    memory_grad_t = memory_grad_t.astype(jnp.bfloat16).reshape(heads, row_width, tokens_here)
+    outgoing = jnp.zeros((devices, row_width, tokens_here), jnp.bfloat16)
+    for head in range(heads):
+        outgoing = jnp.where(owner_t[head] == owners, memory_grad_t[head][None], outgoing)
+    table_grad_t = return_grads(outgoing, wanted_row_list, ngram_table.shape[0])
+    return (layer_out, hidden_grad, table_grad_t.T)
 
 
 def solution(mesh):

time: 293 us -> 201 us (0.69)
  the two profiles are of different devices: /device:TPU:9 before, /device:TPU:25 now
where the time goes in v1:
time: 201 us
  Pallas kernels  145 us (72%)
  other arithmetic  20.9 us (10%)
  local copies, waits for them, and re-layouts  15 us (7%)
  matrix products  8.54 us (4%)
  starting transfers between devices  8.06 us (4%)
  waiting for transfers between devices  2.32 us (1%)
    pallas_call x1, Pallas kernels, fetch(): pl.pallas_call(functools.partial(fetch_kernel, devices), out_shape=(jax.S...  95.9 us
    pallas_call x1, Pallas kernels, return_grads(): pl.pallas_call(functools.partial(return_kernel, devices), out_shape=jax.S...  49.3 us
    unnamed x35, local copies, waits for them, and re-layouts  8.93 us
    ppermute x2, starting transfers between devices, shifted(): return lax.ppermute(value, axis, pairs)  8.06 us
    mul x1, other arithmetic, on_device(): slope = upstream * sigm * (1.0 + mixed * (1.0 - sigm))  6.54 us
    slice x1, local copies, waits for them, and re-layouts, on_device(): keys_proj = contract_first(memory_t, whole[0])  5.77 us
    dot_general x2, matrix products, contract_last(): lax.dot_general(left, right, (((1,), (1,)), ((), ())), preferred_element_...  4.58 us
    reduce_sum x1, other arithmetic, on_device(): jnp.sum(normed_grad * gated, axis=-1, keepdims=True)  4.04 us
  transfers between devices with their start and end apart: 2, of which 2 were waited for; matrix products, arithmetic and copies ran while one was open for 0% of the time, Pallas kernels for 0%

profile of v1, /device:TPU:25, one launch (start us, length us, event | category | flops | bytes accessed | tf_op | source)
XLA Modules:
  0.0 201.1 jit_solution(6474603767435904161)
XLA Ops:
  0.6 0.7 broadcast_compare_fusion.15
  1.4 0.8 select_reduce_fusion
  2.2 0.0 copy-start
  2.2 1.8 copy-done
  4.0 1.0 copy-done.1
  5.0 1.0 copy-done.2
  6.0 95.9 %fetch.1 = (bf16[2,16,80,2560]{3,2,1,0:T(8,128)(2,1)}, bf16[16,160,256]{2,1,0:T(8,128)(2,1)S(1)}, s32[16,1,256]{2,1,0:T(1,128)S(1)}) custom-call(s32[16,1,256]{2,1,0:T(1,128)S(1)} %broadcast_in_dim.398.req, bf16[160,9216]{1,0:T(8,128)(2,1)S(1)} %bitcast.70, bf16[80,2560]{1,0:T(8,128)(2,1)S(1)} %copy-done.1, bf16[80,2560]{1,0:T(8,128)(2,1)S(1)} %copy-done.2), custom_call_target="tpu_custom_call" | custom-call | tf_op jit(solution)/shard_map/fetch/pallas_call | solution.py:205
  101.9 0.1 slice_bitcast_fusion.15
  102.0 0.0 copy-start.7
  102.0 5.8 %fusion.44 = (bf16[1,16,80,2560]{3,2,1,0:T(8,128)(2,1)S(1)}, bf16[1,16,80,2560]{3,2,1,0:T(8,128)(2,1)S(1)}) fusion(bf16[2,16,80,2560]{3,2,1,0:T(8,128)(2,1)} %get-tuple-element.7), kind=kLoop, calls=%fused_computation.134 | loop fusion | bytes 26214400 | tf_op jit(solution)/shard_map/slice | solution.py:310
  107.8 0.0 copy-done.7
  107.8 0.0 copy-start.3
  107.8 0.0 copy-start.4
  107.8 0.3 fusion.20
  108.2 0.8 select_select_fusion.1
  109.0 2.0 multiply_reduce_fusion.3
  110.9 0.0 copy-done.3
  111.0 0.6 fusion.17
  111.6 0.9 copy-done.4
  112.5 2.0 multiply_reduce_fusion.2
  114.5 0.0 copy-start.11
  114.5 0.0 copy-start.12
  114.5 1.5 copy-done.5
  116.0 0.3 multiply_convert_fusion.1
  116.3 0.0 copy-start.9
  116.3 1.0 copy-done.9
  117.4 1.9 collective-permute-start
  119.4 0.0 copy-done.11
  119.4 0.0 copy-done.12
  119.4 0.1 slice_reduce_fusion.3
  119.6 1.2 collective-permute-done
  120.8 6.5 %fusion.18 = (f32[256,2560]{1,0:T(8,128)S(1)}, f32[256,2560]{1,0:T(8,128)S(1)}) fusion(bf16[256,2560]{1,0:T(8,128)(2,1)} %param.9, bf16[256,2560]{1,0:T(8,128)(2,1)} %copy-done.9, bf16[9,2560]{1,0:T(8,128)(2,1)S(1)} %collective-permute-done, pred[256]{0:T(512)(128)(4,1)S(1)} %get-tuple-element.90, f32[2560]{0:T(1024)S(1)} %get-tuple-element.13, ...), kind=kLoop, calls=%fused_computation.29 | loop fusion | flops 21626880 | bytes 7952384 | tf_op jit(solution)/shard_map/mul | solution.py:343
  127.4 6.1 %collective-permute-start.1 = (f32[9,2560]{1,0:T(8,128)S(1)}, f32[9,2560]{1,0:T(8,128)S(1)}, u32[]{:S(2)}, u32[]{:S(2)}) collective-permute-start(f32[9,2560]{1,0:T(8,128)S(1)} %slice.205), channel_id=1, source_target_pairs={{1,0},{2,1},{3,2},{4,3},{5,4},{6,5},{7,6},{8,7},{9,8},{10,9},{11,1... | collective-permute-start | bytes 276488 | tf_op jit(solution)/shard_map/ppermute | solution.py:21
  133.5 1.1 collective-permute-done.1
  134.7 0.0 copy-done.6
  134.7 4.0 %multiply_reduce_fusion.1 = (f32[256]{0:T(256)S(1)}, f32[256,2560]{1,0:T(8,128)S(1)}) fusion(f32[256,2560]{1,0:T(8,128)S(1)} %copy-done.6, f32[256]{0:T(256)S(1)} %add_divide_fusion.1, f32[9,2560]{1,0:T(8,128)S(1)} %collective-permute-done.1, f32[256,2560]{1,0:T(8,128)S(1)} %get-tuple-element.17, pred[256]{0:T(512)(128)(4,1)S(1)} %get-tuple-element.86, ...), kind=kLoop, calls=%fused_computation.42 | loop fusion | flops 11140864 | bytes 8000512 | tf_op jit(solution)/shard_map/reduce_sum | solution.py:356
  138.7 0.0 slice-start
  138.7 0.0 copy-start.8
  138.8 0.0 slice-start.1
  138.8 2.5 %multiply_reduce_fusion = (f32[256]{0:T(256)S(1)}, bf16[256,2560]{1,0:T(8,128)(2,1)}) fusion(f32[256,2560]{1,0:T(8,128)S(1)} %copy-done.6, f32[256]{0:T(256)S(1)} %get-tuple-element.15, f32[256]{0:T(256)S(1)} %add_divide_fusion.1, f32[256]{0:T(256)S(1)} %get-tuple-element.77, f32[256,2560]{1,0:T(8,128)S(1)} %get-tuple-element.16, ...), kind=kLoop, calls=%fused_computation.41 | loop fusion | flops 10485504 | bytes 10490880 | tf_op jit(solution)/shard_map/reduce_sum | solution.py:359
  141.3 1.5 fusion.16
  142.8 0.0 slice-start.3
  142.8 2.2 %fusion.31 = f32[1280,256]{1,0:T(8,128)S(1)} fusion(bf16[1280,2560]{1,0:T(8,128)(2,1)S(1)} %bitcast.74, bf16[256,2560]{1,0:T(8,128)(2,1)S(1)} %copy-done.8, f32[256,2560]{1,0:T(8,128)S(1)} %get-tuple-element.80, f32[256]{0:T(256)S(1)} %get-tuple-element.9, f32[256]{0:T(256)S(1)} %get-tuple-element.72, f32[256]{0:T(256)S(1)} %get-tuple-element.71, ...), kind=kOutput, calls=%fused_computation.54 | convolution fusion | flops 1683619840 | bytes 11801600 | tf_op jit(solution)/shard_map/dot_general | solution.py:29
  145.0 2.4 %fusion.28 = bf16[1280,256]{1,0:T(8,128)(2,1)S(1)} fusion(f32[1280,256]{1,0:T(8,128)S(1)} %fusion.31, bf16[1280,2560]{1,0:T(8,128)(2,1)S(1)} %bitcast.78, f32[256]{0:T(256)S(1)} %add_divide_fusion.1, bf16[256,2560]{1,0:T(8,128)(2,1)S(1)} %copy-done.10, f32[256,2560]{1,0:T(8,128)S(1)} %get-tuple-element.16, f32[256,2560]{1,0:T(8,128)S(1)} %copy-done.6, ...), kind=kOutput, calls=%fused_computation.49 | convolution fusion | flops 1684930560 | bytes 15077376 | tf_op jit(solution)/shard_map/dot_general | solution.py:29
  147.5 0.7 select_select_fusion.out_grads
  148.2 49.3 %return_grads.1 = bf16[160,9216]{1,0:T(8,128)(2,1)S(1)} custom-call(bf16[16,160,256]{2,1,0:T(8,128)(2,1)S(1)} %select_select_fusion.out_grads, s32[16,1,256]{2,1,0:T(1,128)S(1)} %get-tuple-element.8.wanted), custom_call_target="tpu_custom_call" | custom-call | tf_op jit(solution)/shard_map/return_grads/pallas_call | solution.py:279
  197.5 1.9 fusion.24
  199.5 1.6 copy.12
  (31 shorter events, 0.3 us)
Async XLA Ops:
  2.2 1.8 copy-start
  4.0 1.0 copy-start.1
  5.0 1.0 copy-start.2
  102.0 5.8 %copy-start.7 = (bf16[256,2560]{1,0:T(8,128)(2,1)S(1)}, bf16[256,2560]{1,0:T(8,128)(2,1)}, u32[]{:S(2)}) copy-start(bf16[256,2560]{1,0:T(8,128)(2,1)} %param.8) | copy-start | bytes 3932164
  107.8 3.1 %copy-start.3 = (bf16[1,16,80,2560]{3,2,1,0:T(8,128)(2,1)}, bf16[1,16,80,2560]{3,2,1,0:T(8,128)(2,1)S(1)}, u32[]{:S(2)}) copy-start(bf16[1,16,80,2560]{3,2,1,0:T(8,128)(2,1)S(1)} %get-tuple-element.19) | copy-start | bytes 19660804
  107.8 4.7 %copy-start.4 = (bf16[1,16,80,2560]{3,2,1,0:T(8,128)(2,1)}, bf16[1,16,80,2560]{3,2,1,0:T(8,128)(2,1)S(1)}, u32[]{:S(2)}) copy-start(bf16[1,16,80,2560]{3,2,1,0:T(8,128)(2,1)S(1)} %get-tuple-element.20) | copy-start | bytes 19660804
  114.5 1.5 copy-start.5
  114.5 4.9 %copy-start.11 = (s32[256,8]{0,1:T(8,128)S(1)}, s32[256,8]{0,1:T(8,128)}, u32[]{:S(2)}) copy-start(s32[256,8]{0,1:T(8,128)} %param.10) | copy-start | bytes 24580
  114.5 4.9 %copy-start.12 = (f32[4,2560]{1,0:T(4,128)S(1)}, f32[4,2560]{1,0:T(4,128)}, u32[]{:S(2)}) copy-start(f32[4,2560]{1,0:T(4,128)} %param.15) | copy-start | bytes 122884
  116.3 1.1 copy-start.9
  117.4 3.4 %collective-permute-start = (bf16[9,2560]{1,0:T(8,128)(2,1)S(1)}, bf16[9,2560]{1,0:T(8,128)(2,1)S(1)}, u32[]{:S(2)}, u32[]{:S(2)}) collective-permute-start(bf16[9,2560]{1,0:T(8,128)(2,1)S(1)} %slice.200), channel_id=1, source_target_pairs={{0,1},{1,2},{2,3},{3,4},{4,5},{5,6},{6,7},{7,8},{8,9},{9,10},{10,1... | collective-permute-start | bytes 138248 | tf_op jit(solution)/shard_map/ppermute | solution.py:21
  120.8 13.9 %copy-start.6 = (f32[256,2560]{1,0:T(8,128)S(1)}, f32[256,2560]{1,0:T(8,128)}, u32[]{:S(2)}) copy-start(f32[256,2560]{1,0:T(8,128)} %copy-done.5) | copy-start | bytes 7864324
  127.4 7.3 %collective-permute-start.1 = (f32[9,2560]{1,0:T(8,128)S(1)}, f32[9,2560]{1,0:T(8,128)S(1)}, u32[]{:S(2)}, u32[]{:S(2)}) collective-permute-start(f32[9,2560]{1,0:T(8,128)S(1)} %slice.205), channel_id=1, source_target_pairs={{1,0},{2,1},{3,2},{4,3},{5,4},{6,5},{7,6},{8,7},{9,8},{10,9},{11,1... | collective-permute-start | bytes 276488 | tf_op jit(solution)/shard_map/ppermute | solution.py:21
  134.7 4.1 %copy-start.10 = (bf16[256,2560]{1,0:T(8,128)(2,1)S(1)}, bf16[256,2560]{1,0:T(8,128)(2,1)}, u32[]{:S(2)}) copy-start(bf16[256,2560]{1,0:T(8,128)(2,1)} %param.9) | copy-start | bytes 3932164
  138.7 4.0 %slice-start = ((s8[6553600]{0:T(1024)(128)(4,1)}), s8[4194304]{0:T(1024)(128)(4,1)S(1)}, s32[]{:S(2)}) async-start(s8[6553600]{0:T(1024)(128)(4,1)} %bitcast.72), calls=%async_computation | async-start | bytes 8388608
  138.7 2.5 %copy-start.8 = (bf16[256,2560]{1,0:T(8,128)(2,1)S(1)}, bf16[256,2560]{1,0:T(8,128)(2,1)}, u32[]{:S(2)}) copy-start(bf16[256,2560]{1,0:T(8,128)(2,1)} %param.8) | copy-start | bytes 3932164
  138.8 4.0 %slice-start.1 = ((s8[6553600]{0:T(1024)(128)(4,1)}), s8[2359296]{0:T(1024)(128)(4,1)S(1)}, s32[]{:S(2)}) async-start(s8[6553600]{0:T(1024)(128)(4,1)} %bitcast.72), calls=%async_computation.1 | async-start | bytes 4718592
  141.3 3.7 %slice-start.2 = ((s8[6553600]{0:T(1024)(128)(4,1)}), s8[4194304]{0:T(1024)(128)(4,1)S(1)}, s32[]{:S(2)}) async-start(s8[6553600]{0:T(1024)(128)(4,1)} %bitcast.76), calls=%async_computation.2 | async-start | bytes 8388608
  142.8 2.2 %slice-start.3 = ((s8[6553600]{0:T(1024)(128)(4,1)}), s8[2359296]{0:T(1024)(128)(4,1)S(1)}, s32[]{:S(2)}) async-start(s8[6553600]{0:T(1024)(128)(4,1)} %bitcast.76), calls=%async_computation.3 | async-start | bytes 4718592

commit v2 on v1

--- a/solution.py
+++ b/solution.py
@@ -41,7 +41,7 @@
 MESH = pl.DeviceIdType.MESH
 
 
-def enter(group, me, devices):
+def enter(group, me, devices, twin=None):
     barrier = pltpu.get_barrier_semaphore()
 
     def greet(i, carry):
@@ -51,7 +51,9 @@
         return carry
 
     lax.fori_loop(1, devices, greet, 0)
-    pl.semaphore_wait(barrier, devices - 1)
+    if twin is not None:
+        pl.semaphore_signal(barrier, inc=1, device_id=(twin, me), device_id_type=MESH)
+    pl.semaphore_wait(barrier, devices - 1 if twin is None else devices)
 
 
 def picks(slots, start, rows):
@@ -65,8 +67,9 @@
 
 
 def fetch_kernel(
-    devices, req, tab, wk, wv, weights, replies, wanted, out_rows,
-    ring_send, ring_recv, core_send, core_recv, req_send, req_recv, rep_send, rep_recv, own_sem,
+    devices, req, tab_hbm, wk, wv, weights, replies, wanted, tab, out_rows,
+    ring_send, ring_recv, core_send, core_recv, twin_send, twin_recv,
+    req_send, req_recv, rep_send, rep_recv, own_sem,
 ):
     group, me = lax.axis_index("groups"), lax.axis_index("table")
     chips = devices // 2
@@ -74,6 +77,8 @@
     core, chip = me % 2, me // 2
     odd = chip % 2
     pos = (1 - odd) * (chip // 2) + odd * (chips - 1 - chip // 2)
+    mine = group % 2
+    twin = group + 1 - 2 * mine
 
     def at_ring(r):
         r = (r + 2 * chips) % chips
@@ -83,33 +88,39 @@
     partner = me + 1 - 2 * core
     ways = (at_ring(pos + 1), at_ring(pos - 1))
     half = wk.shape[1] // 2
-    parts = (wk, wv)
-
-    def block(d, kv, origin):
+
+    def block(d, kv, s):
+        origin = at_ring(pos - (1 - 2 * d) * s)
         return weights.at[kv, origin, :, pl.ds(d * half, half)]
 
-    def ring_copy(d, kv, s):
-        sign = 1 - 2 * d
-        origin = at_ring(pos - sign * s)
-        source = parts[kv].at[:, pl.ds(d * half, half)] if s == 0 else block(d, kv, origin)
+    def block_copy(ref, send_sem, recv_sem, to):
         return pltpu.make_async_remote_copy(
-            src_ref=source, dst_ref=block(d, kv, origin),
-            send_sem=ring_send.at[d, kv, s], recv_sem=ring_recv.at[d, kv, s],
-            device_id=(group, ways[d]), device_id_type=MESH,
-        )
-
-    def core_copy(d, kv, s):
-        sign = 1 - 2 * d
-        origin = at_ring(pos - sign * s)
-        source = parts[kv].at[:, pl.ds(d * half, half)] if s == 0 else block(d, kv, origin)
-        return pltpu.make_async_remote_copy(
-            src_ref=source, dst_ref=block(d, kv, origin),
-            send_sem=core_send.at[d, kv, s], recv_sem=core_recv.at[d, kv, s],
-            device_id=(group, partner), device_id_type=MESH,
+            src_ref=ref, dst_ref=ref, send_sem=send_sem, recv_sem=recv_sem,
+            device_id=to, device_id_type=MESH,
+        )
+
+    def ring_copy(d, s):
+        return block_copy(
+            block(d, mine, s), ring_send.at[d, s], ring_recv.at[d, s], (group, ways[d])
+        )
+
+    def twin_copy(d, s):
+        return block_copy(
+            block(d, mine, s), twin_send.at[d, s], twin_recv.at[d, s], (twin, me)
+        )
+
+    def core_copy(d, other, s):
+        kv = 1 - mine if other else mine
+        return block_copy(
+            block(d, kv, s), core_send.at[d, other, s], core_recv.at[d, other, s],
+            (group, partner),
         )
 
     def own_copy(kv):
-        return pltpu.make_async_copy(parts[kv], weights.at[kv, me], own_sem.at[kv])
+        return pltpu.make_async_copy((wk, wv)[kv], weights.at[kv, me], own_sem.at[kv])
+
+    def tab_copy():
+        return pltpu.make_async_copy(tab_hbm, tab, own_sem.at[2])
 
     def req_copy(i):
         to = lax.rem(me + i, devices)
@@ -127,7 +138,10 @@
             device_id=(group, to), device_id_type=MESH,
         )
 
-    enter(group, me, devices)
+    for kv in range(2):
+        own_copy(kv).start()
+    tab_copy().start()
+    enter(group, me, devices, twin)
 
     def send_request(i, carry):
         req_copy(i).start()
@@ -135,20 +149,26 @@
 
     lax.fori_loop(1, devices, send_request, 0)
     for kv in range(2):
+        own_copy(kv).wait()
+    for d in range(2):
+        ring_copy(d, 0).start()
+    for d in range(2):
+        for other in range(2):
+            core_copy(d, other, 0).start()
+    tab_copy().wait()
+
+    def pass_on(s):
         for d in range(2):
-            ring_copy(d, kv, 0).start()
-    for kv in range(2):
-        own_copy(kv).start()
+            ring_copy(d, s).wait_recv()
+            if s < chips - 2:
+                ring_copy(d, s + 1).start()
+            twin_copy(d, s + 1).start()
+            core_copy(d, 0, s + 1).start()
+
+    def share(s):
         for d in range(2):
-            core_copy(d, kv, 0).start()
-
-    def pass_on(s):
-        for kv in range(2):
-            for d in range(2):
-                ring_copy(d, kv, s).wait_recv()
-                if s < chips - 2:
-                    ring_copy(d, kv, s + 1).start()
-                core_copy(d, kv, s + 1).start()
+            twin_copy(d, s).wait_recv()
+            core_copy(d, 1, s).start()
 
     def look_up(slots):
         total = None
@@ -167,16 +187,22 @@
         rep_copy(i).start()
         return carry
 
-    first, second = devices * 3 // 8, devices * 3 // 4
-    lax.fori_loop(1, first, answer, 0)
-    pass_on(0)
-    lax.fori_loop(first, second, answer, 0)
-    pass_on(1)
-    lax.fori_loop(second, devices, answer, 0)
+    bounds = [1] + [devices * j // 4 for j in range(1, 5)]
+    stages = min(4, chips - 1)
+    for j in range(4):
+        lax.fori_loop(bounds[j], bounds[j + 1], answer, 0)
+        if j < 3 and j < stages - 1:
+            pass_on(j)
+    pass_on(stages - 1)
     wanted[me] = req[me]
     replies[me] = look_up(req[me])
-    for s in range(2, chips - 1):
+    shared = 1
+    for s in range(stages, chips - 1):
         pass_on(s)
+        share(shared)
+        shared += 1
+    for s in range(shared, chips):
+        share(s)
 
     def finish(i, carry):
         req_copy(i).wait_send()
@@ -185,14 +211,15 @@
         return carry
 
     lax.fori_loop(1, devices, finish, 0)
-    for kv in range(2):
-        own_copy(kv).wait()
-        for d in range(2):
-            for s in range(chips):
-                if s < chips - 1:
-                    ring_copy(d, kv, s).wait_send()
-                core_copy(d, kv, s).wait_send()
-                core_copy(d, kv, s).wait_recv()
+    for d in range(2):
+        for s in range(chips):
+            if s < chips - 1:
+                ring_copy(d, s).wait_send()
+            if s > 0:
+                twin_copy(d, s).wait_send()
+            for other in range(2):
+                core_copy(d, other, s).wait_send()
+                core_copy(d, other, s).wait_recv()
 
 
 def fetch(requests, table_t, w_key, w_value):
@@ -209,12 +236,14 @@
             jax.ShapeDtypeStruct((devices, row_width, tokens), jnp.bfloat16),
             jax.ShapeDtypeStruct((devices, 1, tokens), jnp.int32),
         ),
-        in_specs=[vmem, vmem, hbm, hbm],
+        in_specs=[vmem, hbm, hbm, hbm],
         out_specs=(hbm, vmem, vmem),
         scratch_shapes=[
+            pltpu.VMEM(table_t.shape, jnp.bfloat16),
             pltpu.VMEM((devices, row_width, tokens), jnp.bfloat16),
-            dma((2, 2, chips)), dma((2, 2, chips)), dma((2, 2, chips)), dma((2, 2, chips)),
-            dma((devices,)), dma((devices,)), dma((devices,)), dma((devices,)), dma((2,)),
+            dma((2, chips)), dma((2, chips)), dma((2, 2, chips)), dma((2, 2, chips)),
+            dma((2, chips)), dma((2, chips)),
+            dma((devices,)), dma((devices,)), dma((devices,)), dma((devices,)), dma((3,)),
         ],
         compiler_params=pltpu.CompilerParams(
             collective_id=0, has_side_effects=True, vmem_limit_bytes=48 * 1024 * 1024

time: 201 us -> 195 us (0.970)
  Pallas kernels: 145 us -> 139 us
    pallas_call x1, Pallas kernels: 95.9 us -> 86.2 us  [fetch(): pl.pallas_call(functools.partial(fetch_kernel, devices), out_shape=(jax.S...]
    pallas_call x1, Pallas kernels: 49.3 us -> 52.6 us  [return_grads(): pl.pallas_call(functools.partial(return_kernel, devices), out_shape=jax.S...]
where the time goes in v2:
time: 195 us
  Pallas kernels  139 us (71%)
  other arithmetic  20.9 us (11%)
  local copies, waits for them, and re-layouts  15 us (8%)
  matrix products  8.54 us (4%)
  starting transfers between devices  7.42 us (4%)
  waiting for transfers between devices  2.95 us (2%)
    pallas_call x1, Pallas kernels, fetch(): pl.pallas_call(functools.partial(fetch_kernel, devices), out_shape=(jax.S...  86.2 us
    pallas_call x1, Pallas kernels, return_grads(): pl.pallas_call(functools.partial(return_kernel, devices), out_shape=jax.S...  52.6 us
    unnamed x35, local copies, waits for them, and re-layouts  8.93 us
    ppermute x2, starting transfers between devices, shifted(): return lax.ppermute(value, axis, pairs)  7.42 us
    mul x1, other arithmetic, on_device(): slope = upstream * sigm * (1.0 + mixed * (1.0 - sigm))  6.54 us
    slice x1, local copies, waits for them, and re-layouts, on_device(): keys_proj = contract_first(memory_t, whole[0])  5.77 us
    dot_general x2, matrix products, contract_last(): lax.dot_general(left, right, (((1,), (1,)), ((), ())), preferred_element_...  4.58 us
    reduce_sum x1, other arithmetic, on_device(): jnp.sum(normed_grad * gated, axis=-1, keepdims=True)  4.04 us
  transfers between devices with their start and end apart: 2, of which 2 were waited for; matrix products, arithmetic and copies ran while one was open for 0% of the time, Pallas kernels for 0%

profile of v2, /device:TPU:25, one launch (start us, length us, event | category | flops | bytes accessed | tf_op | source)
XLA Modules:
  0.0 194.6 jit_solution(8953341922171399363)
XLA Ops:
  0.6 0.7 broadcast_compare_fusion.15
  1.4 0.8 select_reduce_fusion
  2.2 0.0 copy-start
  2.2 1.8 copy-done
  4.0 1.0 copy-done.1
  5.0 1.0 copy-done.2
  6.0 86.2 %fetch.1 = (bf16[2,16,80,2560]{3,2,1,0:T(8,128)(2,1)}, bf16[16,160,256]{2,1,0:T(8,128)(2,1)S(1)}, s32[16,1,256]{2,1,0:T(1,128)S(1)}) custom-call(s32[16,1,256]{2,1,0:T(1,128)S(1)} %broadcast_in_dim.398.req, bf16[160,9216]{1,0:T(8,128)(2,1)S(1)} %bitcast.70, bf16[80,2560]{1,0:T(8,128)(2,1)S(1)} %copy-done.1, bf16[80,2560]{1,0:T(8,128)(2,1)S(1)} %copy-done.2), custom_call_target="tpu_custom_call" | custom-call | tf_op jit(solution)/shard_map/fetch/pallas_call | solution.py:232
  92.2 0.1 slice_bitcast_fusion.15
  92.3 0.0 copy-start.7
  92.3 5.8 %fusion.44 = (bf16[1,16,80,2560]{3,2,1,0:T(8,128)(2,1)S(1)}, bf16[1,16,80,2560]{3,2,1,0:T(8,128)(2,1)S(1)}) fusion(bf16[2,16,80,2560]{3,2,1,0:T(8,128)(2,1)} %get-tuple-element.7), kind=kLoop, calls=%fused_computation.134 | loop fusion | bytes 26214400 | tf_op jit(solution)/shard_map/slice | solution.py:339
  98.1 0.0 copy-done.7
  98.1 0.0 copy-start.3
  98.1 0.0 copy-start.4
  98.1 0.3 fusion.20
  98.4 0.8 select_select_fusion.1
  99.2 2.0 %multiply_reduce_fusion.3 = (f32[256]{0:T(256)S(1)}, f32[256,2560]{1,0:T(8,128)S(1)}) fusion(bf16[1280,256]{1,0:T(8,128)(2,1)S(1)} %bitcast.79, bf16[1280,2560]{1,0:T(8,128)(2,1)S(1)} %bitcast.71), kind=kOutput, calls=%fused_computation.48 | convolution fusion | flops 1679032064 | bytes 9831424 | tf_op jit(solution)/shard_map/dot_general | solution.py:35
  101.2 0.0 copy-done.3
  101.2 0.6 fusion.17
  101.8 0.9 copy-done.4
  102.7 2.0 %multiply_reduce_fusion.2 = (f32[256]{0:T(256)S(1)}, f32[256,2560]{1,0:T(8,128)S(1)}) fusion(f32[256]{0:T(256)S(1)} %add_divide_fusion.1, bf16[1280,256]{1,0:T(8,128)(2,1)S(1)} %bitcast.80, bf16[1280,2560]{1,0:T(8,128)(2,1)S(1)} %bitcast.75), kind=kOutput, calls=%fused_computation.47 | convolution fusion | flops 1679687424 | bytes 9832448 | tf_op jit(solution)/shard_map/dot_general | solution.py:35
  104.7 0.0 copy-start.11
  104.8 0.0 copy-start.12
  104.8 1.5 copy-done.5
  106.2 0.3 multiply_convert_fusion.1
  106.6 0.0 copy-start.9
  106.6 1.0 copy-done.9
  107.7 1.9 collective-permute-start
  109.6 0.0 copy-done.11
  109.6 0.0 copy-done.12
  109.7 0.1 slice_reduce_fusion.3
  109.9 1.2 collective-permute-done
  111.0 6.5 %fusion.18 = (f32[256,2560]{1,0:T(8,128)S(1)}, f32[256,2560]{1,0:T(8,128)S(1)}) fusion(bf16[256,2560]{1,0:T(8,128)(2,1)} %param.9, bf16[256,2560]{1,0:T(8,128)(2,1)} %copy-done.9, bf16[9,2560]{1,0:T(8,128)(2,1)S(1)} %collective-permute-done, pred[256]{0:T(512)(128)(4,1)S(1)} %get-tuple-element.90, f32[2560]{0:T(1024)S(1)} %get-tuple-element.13, ...), kind=kLoop, calls=%fused_computation.29 | loop fusion | flops 21626880 | bytes 7952384 | tf_op jit(solution)/shard_map/mul | solution.py:372
  117.6 5.5 %collective-permute-start.1 = (f32[9,2560]{1,0:T(8,128)S(1)}, f32[9,2560]{1,0:T(8,128)S(1)}, u32[]{:S(2)}, u32[]{:S(2)}) collective-permute-start(f32[9,2560]{1,0:T(8,128)S(1)} %slice.205), channel_id=1, source_target_pairs={{1,0},{2,1},{3,2},{4,3},{5,4},{6,5},{7,6},{8,7},{9,8},{10,9},{11,1... | collective-permute-start | bytes 276488 | tf_op jit(solution)/shard_map/ppermute | solution.py:21
  123.1 1.8 collective-permute-done.1
  124.9 4.0 %multiply_reduce_fusion.1 = (f32[256]{0:T(256)S(1)}, f32[256,2560]{1,0:T(8,128)S(1)}) fusion(f32[256,2560]{1,0:T(8,128)S(1)} %copy-done.6, f32[256]{0:T(256)S(1)} %add_divide_fusion.1, f32[9,2560]{1,0:T(8,128)S(1)} %collective-permute-done.1, f32[256,2560]{1,0:T(8,128)S(1)} %get-tuple-element.17, pred[256]{0:T(512)(128)(4,1)S(1)} %get-tuple-element.86, ...), kind=kLoop, calls=%fused_computation.42 | loop fusion | flops 11140864 | bytes 8000512 | tf_op jit(solution)/shard_map/reduce_sum | solution.py:385
  129.0 0.0 slice-start
  129.0 0.0 copy-start.8
  129.0 0.0 slice-start.1
  129.0 2.5 %multiply_reduce_fusion = (f32[256]{0:T(256)S(1)}, bf16[256,2560]{1,0:T(8,128)(2,1)}) fusion(f32[256,2560]{1,0:T(8,128)S(1)} %copy-done.6, f32[256]{0:T(256)S(1)} %get-tuple-element.15, f32[256]{0:T(256)S(1)} %add_divide_fusion.1, f32[256]{0:T(256)S(1)} %get-tuple-element.77, f32[256,2560]{1,0:T(8,128)S(1)} %get-tuple-element.16, ...), kind=kLoop, calls=%fused_computation.41 | loop fusion | flops 10485504 | bytes 10490880 | tf_op jit(solution)/shard_map/reduce_sum | solution.py:388
  131.5 0.0 copy-done.8
  131.5 1.5 fusion.16
  133.0 0.0 slice-start.3
  133.0 2.2 %fusion.31 = f32[1280,256]{1,0:T(8,128)S(1)} fusion(bf16[1280,2560]{1,0:T(8,128)(2,1)S(1)} %bitcast.74, bf16[256,2560]{1,0:T(8,128)(2,1)S(1)} %copy-done.8, f32[256,2560]{1,0:T(8,128)S(1)} %get-tuple-element.80, f32[256]{0:T(256)S(1)} %get-tuple-element.9, f32[256]{0:T(256)S(1)} %get-tuple-element.72, f32[256]{0:T(256)S(1)} %get-tuple-element.71, ...), kind=kOutput, calls=%fused_computation.54 | convolution fusion | flops 1683619840 | bytes 11801600 | tf_op jit(solution)/shard_map/dot_general | solution.py:29
  135.3 2.4 %fusion.28 = bf16[1280,256]{1,0:T(8,128)(2,1)S(1)} fusion(f32[1280,256]{1,0:T(8,128)S(1)} %fusion.31, bf16[1280,2560]{1,0:T(8,128)(2,1)S(1)} %bitcast.78, f32[256]{0:T(256)S(1)} %add_divide_fusion.1, bf16[256,2560]{1,0:T(8,128)(2,1)S(1)} %copy-done.10, f32[256,2560]{1,0:T(8,128)S(1)} %get-tuple-element.16, f32[256,2560]{1,0:T(8,128)S(1)} %copy-done.6, ...), kind=kOutput, calls=%fused_computation.49 | convolution fusion | flops 1684930560 | bytes 15077376 | tf_op jit(solution)/shard_map/dot_general | solution.py:29
  137.7 0.7 select_select_fusion.out_grads
  138.5 52.6 %return_grads.1 = bf16[160,9216]{1,0:T(8,128)(2,1)S(1)} custom-call(bf16[16,160,256]{2,1,0:T(8,128)(2,1)S(1)} %select_select_fusion.out_grads, s32[16,1,256]{2,1,0:T(1,128)S(1)} %get-tuple-element.8.wanted), custom_call_target="tpu_custom_call" | custom-call | tf_op jit(solution)/shard_map/return_grads/pallas_call | solution.py:308
  191.0 1.9 %fusion.24 = bf16[256,2560]{1,0:T(8,128)(2,1)} fusion(bf16[256,2560]{1,0:T(8,128)(2,1)S(1)} %copy-done.8, f32[256,2560]{1,0:T(8,128)S(1)} %get-tuple-element.80, f32[256]{0:T(256)S(1)} %get-tuple-element.10, f32[256]{0:T(256)S(1)} %get-tuple-element.84, f32[256]{0:T(256)S(1)} %get-tuple-element.85, f32[256]{0:T(256)S(1)} %subtract_multiply_fusion, ...), kind=kLoop, calls=%fused_computation.35 | loop fusion | flops 5898240 | bytes 5248000 | tf_op jit(solution)/shard_map/convert_element_type | solution.py:404
  193.0 1.6 copy.12
  (31 shorter events, 0.3 us)
Async XLA Ops:
  2.2 1.8 copy-start
  4.0 1.0 copy-start.1
  5.0 1.0 copy-start.2
  92.3 5.8 %copy-start.7 = (bf16[256,2560]{1,0:T(8,128)(2,1)S(1)}, bf16[256,2560]{1,0:T(8,128)(2,1)}, u32[]{:S(2)}) copy-start(bf16[256,2560]{1,0:T(8,128)(2,1)} %param.8) | copy-start | bytes 3932164
  98.1 3.1 %copy-start.3 = (bf16[1,16,80,2560]{3,2,1,0:T(8,128)(2,1)}, bf16[1,16,80,2560]{3,2,1,0:T(8,128)(2,1)S(1)}, u32[]{:S(2)}) copy-start(bf16[1,16,80,2560]{3,2,1,0:T(8,128)(2,1)S(1)} %get-tuple-element.19) | copy-start | bytes 19660804
  98.1 4.7 %copy-start.4 = (bf16[1,16,80,2560]{3,2,1,0:T(8,128)(2,1)}, bf16[1,16,80,2560]{3,2,1,0:T(8,128)(2,1)S(1)}, u32[]{:S(2)}) copy-start(bf16[1,16,80,2560]{3,2,1,0:T(8,128)(2,1)S(1)} %get-tuple-element.20) | copy-start | bytes 19660804
  104.7 1.5 copy-start.5
  104.7 4.9 %copy-start.11 = (s32[256,8]{0,1:T(8,128)S(1)}, s32[256,8]{0,1:T(8,128)}, u32[]{:S(2)}) copy-start(s32[256,8]{0,1:T(8,128)} %param.10) | copy-start | bytes 24580
  104.8 4.9 %copy-start.12 = (f32[4,2560]{1,0:T(4,128)S(1)}, f32[4,2560]{1,0:T(4,128)}, u32[]{:S(2)}) copy-start(f32[4,2560]{1,0:T(4,128)} %param.15) | copy-start | bytes 122884
  106.6 1.1 copy-start.9
  107.7 3.4 %collective-permute-start = (bf16[9,2560]{1,0:T(8,128)(2,1)S(1)}, bf16[9,2560]{1,0:T(8,128)(2,1)S(1)}, u32[]{:S(2)}, u32[]{:S(2)}) collective-permute-start(bf16[9,2560]{1,0:T(8,128)(2,1)S(1)} %slice.200), channel_id=1, source_target_pairs={{0,1},{1,2},{2,3},{3,4},{4,5},{5,6},{6,7},{7,8},{8,9},{9,10},{10,1... | collective-permute-start | bytes 138248 | tf_op jit(solution)/shard_map/ppermute | solution.py:21
  111.0 13.9 %copy-start.6 = (f32[256,2560]{1,0:T(8,128)S(1)}, f32[256,2560]{1,0:T(8,128)}, u32[]{:S(2)}) copy-start(f32[256,2560]{1,0:T(8,128)} %copy-done.5) | copy-start | bytes 7864324
  117.6 7.3 %collective-permute-start.1 = (f32[9,2560]{1,0:T(8,128)S(1)}, f32[9,2560]{1,0:T(8,128)S(1)}, u32[]{:S(2)}, u32[]{:S(2)}) collective-permute-start(f32[9,2560]{1,0:T(8,128)S(1)} %slice.205), channel_id=1, source_target_pairs={{1,0},{2,1},{3,2},{4,3},{5,4},{6,5},{7,6},{8,7},{9,8},{10,9},{11,1... | collective-permute-start | bytes 276488 | tf_op jit(solution)/shard_map/ppermute | solution.py:21
  124.9 4.1 %copy-start.10 = (bf16[256,2560]{1,0:T(8,128)(2,1)S(1)}, bf16[256,2560]{1,0:T(8,128)(2,1)}, u32[]{:S(2)}) copy-start(bf16[256,2560]{1,0:T(8,128)(2,1)} %param.9) | copy-start | bytes 3932164
  129.0 4.0 %slice-start = ((s8[6553600]{0:T(1024)(128)(4,1)}), s8[4194304]{0:T(1024)(128)(4,1)S(1)}, s32[]{:S(2)}) async-start(s8[6553600]{0:T(1024)(128)(4,1)} %bitcast.72), calls=%async_computation | async-start | bytes 8388608
  129.0 2.5 %copy-start.8 = (bf16[256,2560]{1,0:T(8,128)(2,1)S(1)}, bf16[256,2560]{1,0:T(8,128)(2,1)}, u32[]{:S(2)}) copy-start(bf16[256,2560]{1,0:T(8,128)(2,1)} %param.8) | copy-start | bytes 3932164
  129.0 4.0 %slice-start.1 = ((s8[6553600]{0:T(1024)(128)(4,1)}), s8[2359296]{0:T(1024)(128)(4,1)S(1)}, s32[]{:S(2)}) async-start(s8[6553600]{0:T(1024)(128)(4,1)} %bitcast.72), calls=%async_computation.1 | async-start | bytes 4718592
  131.5 3.7 %slice-start.2 = ((s8[6553600]{0:T(1024)(128)(4,1)}), s8[4194304]{0:T(1024)(128)(4,1)S(1)}, s32[]{:S(2)}) async-start(s8[6553600]{0:T(1024)(128)(4,1)} %bitcast.76), calls=%async_computation.2 | async-start | bytes 8388608
  133.0 2.2 %slice-start.3 = ((s8[6553600]{0:T(1024)(128)(4,1)}), s8[2359296]{0:T(1024)(128)(4,1)S(1)}, s32[]{:S(2)}) async-start(s8[6553600]{0:T(1024)(128)(4,1)} %bitcast.76), calls=%async_computation.3 | async-start | bytes 4718592

commit v3 on v2

--- a/solution.py
+++ b/solution.py
@@ -187,17 +187,20 @@
         rep_copy(i).start()
         return carry
 
-    bounds = [1] + [devices * j // 4 for j in range(1, 5)]
-    stages = min(4, chips - 1)
-    for j in range(4):
+    bounds = [1] + [devices * j // 8 for j in range(1, 9)]
+    passed, shared = 1, 1
+    pass_on(0)
+    for j in range(8):
         lax.fori_loop(bounds[j], bounds[j + 1], answer, 0)
-        if j < 3 and j < stages - 1:
-            pass_on(j)
-    pass_on(stages - 1)
+        if passed < chips - 1:
+            pass_on(passed)
+            passed += 1
+        if j in (3, 5, 7) and shared < passed:
+            share(shared)
+            shared += 1
     wanted[me] = req[me]
     replies[me] = look_up(req[me])
-    shared = 1
-    for s in range(stages, chips - 1):
+    for s in range(passed, chips - 1):
         pass_on(s)
         share(shared)
         shared += 1

time: 195 us -> 181 us (0.928)
  Pallas kernels: 139 us -> 125 us
    pallas_call x1, Pallas kernels: 86.2 us -> 76.9 us  [fetch(): pl.pallas_call(functools.partial(fetch_kernel, devices), out_shape=(jax.S...]
    pallas_call x1, Pallas kernels: 52.6 us -> 47.8 us  [return_grads(): pl.pallas_call(functools.partial(return_kernel, devices), out_shape=jax.S...]
where the time goes in v3:
time: 181 us
  Pallas kernels  125 us (69%)
  other arithmetic  20.9 us (12%)
  local copies, waits for them, and re-layouts  15.2 us (8%)
  matrix products  8.54 us (5%)
  starting transfers between devices  7.24 us (4%)
  waiting for transfers between devices  3.4 us (2%)
    pallas_call x1, Pallas kernels, fetch(): pl.pallas_call(functools.partial(fetch_kernel, devices), out_shape=(jax.S...  76.9 us
    pallas_call x1, Pallas kernels, return_grads(): pl.pallas_call(functools.partial(return_kernel, devices), out_shape=jax.S...  47.8 us
    unnamed x35, local copies, waits for them, and re-layouts  8.93 us
    ppermute x2, starting transfers between devices, shifted(): return lax.ppermute(value, axis, pairs)  7.24 us
    mul x1, other arithmetic, on_device(): slope = upstream * sigm * (1.0 + mixed * (1.0 - sigm))  6.54 us
    slice x1, local copies, waits for them, and re-layouts, on_device(): keys_proj = contract_first(memory_t, whole[0])  5.95 us
    dot_general x2, matrix products, contract_last(): lax.dot_general(left, right, (((1,), (1,)), ((), ())), preferred_element_...  4.58 us
    reduce_sum x1, other arithmetic, on_device(): jnp.sum(normed_grad * gated, axis=-1, keepdims=True)  4.04 us
  transfers between devices with their start and end apart: 2, of which 2 were waited for; matrix products, arithmetic and copies ran while one was open for 0% of the time, Pallas kernels for 0%

profile of v3, /device:TPU:25, one launch (start us, length us, event | category | flops | bytes accessed | tf_op | source)
XLA Modules:
  0.0 181.0 jit_solution(335703473041000231)
XLA Ops:
  0.6 0.7 broadcast_compare_fusion.15
  1.4 0.8 select_reduce_fusion
  2.2 0.0 copy-start
  2.2 1.8 %copy-done = bf16[9216,160]{0,1:T(8,128)(2,1)S(1)} copy-done((bf16[9216,160]{0,1:T(8,128)(2,1)S(1)}, bf16[9216,160]{0,1:T(8,128)(2,1)}, u32[]{:S(2)}) %copy-start) | copy-done | bytes 2949144
  4.0 1.0 copy-done.1
  5.0 1.0 copy-done.2
  6.0 76.9 %fetch.1 = (bf16[2,16,80,2560]{3,2,1,0:T(8,128)(2,1)}, bf16[16,160,256]{2,1,0:T(8,128)(2,1)S(1)}, s32[16,1,256]{2,1,0:T(1,128)S(1)}) custom-call(s32[16,1,256]{2,1,0:T(1,128)S(1)} %broadcast_in_dim.398.req, bf16[160,9216]{1,0:T(8,128)(2,1)S(1)} %bitcast.70, bf16[80,2560]{1,0:T(8,128)(2,1)S(1)} %copy-done.1, bf16[80,2560]{1,0:T(8,128)(2,1)S(1)} %copy-done.2), custom_call_target="tpu_custom_call" | custom-call | tf_op jit(solution)/shard_map/fetch/pallas_call | solution.py:235
  82.9 0.1 slice_bitcast_fusion.15
  83.0 0.0 copy-start.7
  83.0 6.0 %fusion.44 = (bf16[1,16,80,2560]{3,2,1,0:T(8,128)(2,1)S(1)}, bf16[1,16,80,2560]{3,2,1,0:T(8,128)(2,1)S(1)}) fusion(bf16[2,16,80,2560]{3,2,1,0:T(8,128)(2,1)} %get-tuple-element.7), kind=kLoop, calls=%fused_computation.134 | loop fusion | bytes 26214400 | tf_op jit(solution)/shard_map/slice | solution.py:342
  88.9 0.0 copy-done.7
  89.0 0.0 copy-start.3
  89.0 0.0 copy-start.4
  89.0 0.3 fusion.20
  89.3 0.8 select_select_fusion.1
  90.1 2.0 %multiply_reduce_fusion.3 = (f32[256]{0:T(256)S(1)}, f32[256,2560]{1,0:T(8,128)S(1)}) fusion(bf16[1280,256]{1,0:T(8,128)(2,1)S(1)} %bitcast.79, bf16[1280,2560]{1,0:T(8,128)(2,1)S(1)} %bitcast.71), kind=kOutput, calls=%fused_computation.48 | convolution fusion | flops 1679032064 | bytes 9831424 | tf_op jit(solution)/shard_map/dot_general | solution.py:35
  92.1 0.0 copy-done.3
  92.1 0.6 fusion.17
  92.7 0.9 copy-done.4
  93.6 2.0 %multiply_reduce_fusion.2 = (f32[256]{0:T(256)S(1)}, f32[256,2560]{1,0:T(8,128)S(1)}) fusion(f32[256]{0:T(256)S(1)} %add_divide_fusion.1, bf16[1280,256]{1,0:T(8,128)(2,1)S(1)} %bitcast.80, bf16[1280,2560]{1,0:T(8,128)(2,1)S(1)} %bitcast.75), kind=kOutput, calls=%fused_computation.47 | convolution fusion | flops 1679687424 | bytes 9832448 | tf_op jit(solution)/shard_map/dot_general | solution.py:35
  95.6 0.0 copy-start.11
  95.6 0.0 copy-start.12
  95.7 1.5 copy-done.5
  97.1 0.3 multiply_convert_fusion.1
  97.4 0.0 copy-start.9
  97.5 1.0 copy-done.9
  98.5 2.2 %collective-permute-start = (bf16[9,2560]{1,0:T(8,128)(2,1)S(1)}, bf16[9,2560]{1,0:T(8,128)(2,1)S(1)}, u32[]{:S(2)}, u32[]{:S(2)}) collective-permute-start(bf16[9,2560]{1,0:T(8,128)(2,1)S(1)} %slice.200), channel_id=1, source_target_pairs={{0,1},{1,2},{2,3},{3,4},{4,5},{5,6},{6,7},{7,8},{8,9},{9,10},{10,1... | collective-permute-start | bytes 138248 | tf_op jit(solution)/shard_map/ppermute | solution.py:21
  100.8 0.0 copy-done.11
  100.8 0.0 copy-done.12
  100.8 0.1 slice_reduce_fusion.3
  101.0 1.2 collective-permute-done
  102.2 6.5 %fusion.18 = (f32[256,2560]{1,0:T(8,128)S(1)}, f32[256,2560]{1,0:T(8,128)S(1)}) fusion(bf16[256,2560]{1,0:T(8,128)(2,1)} %param.9, bf16[256,2560]{1,0:T(8,128)(2,1)} %copy-done.9, bf16[9,2560]{1,0:T(8,128)(2,1)S(1)} %collective-permute-done, pred[256]{0:T(512)(128)(4,1)S(1)} %get-tuple-element.90, f32[2560]{0:T(1024)S(1)} %get-tuple-element.13, ...), kind=kLoop, calls=%fused_computation.29 | loop fusion | flops 21626880 | bytes 7952384 | tf_op jit(solution)/shard_map/mul | solution.py:375
  108.8 5.0 %collective-permute-start.1 = (f32[9,2560]{1,0:T(8,128)S(1)}, f32[9,2560]{1,0:T(8,128)S(1)}, u32[]{:S(2)}, u32[]{:S(2)}) collective-permute-start(f32[9,2560]{1,0:T(8,128)S(1)} %slice.205), channel_id=1, source_target_pairs={{1,0},{2,1},{3,2},{4,3},{5,4},{6,5},{7,6},{8,7},{9,8},{10,9},{11,1... | collective-permute-start | bytes 276488 | tf_op jit(solution)/shard_map/ppermute | solution.py:21
  113.8 2.2 %collective-permute-done.1 = f32[9,2560]{1,0:T(8,128)S(1)} collective-permute-done((f32[9,2560]{1,0:T(8,128)S(1)}, f32[9,2560]{1,0:T(8,128)S(1)}, u32[]{:S(2)}, u32[]{:S(2)}) %collective-permute-start.1) | collective-permute-done | bytes 92192 | tf_op jit(solution)/shard_map/ppermute | solution.py:21
  116.1 0.0 copy-done.6
  116.1 4.0 %multiply_reduce_fusion.1 = (f32[256]{0:T(256)S(1)}, f32[256,2560]{1,0:T(8,128)S(1)}) fusion(f32[256,2560]{1,0:T(8,128)S(1)} %copy-done.6, f32[256]{0:T(256)S(1)} %add_divide_fusion.1, f32[9,2560]{1,0:T(8,128)S(1)} %collective-permute-done.1, f32[256,2560]{1,0:T(8,128)S(1)} %get-tuple-element.17, pred[256]{0:T(512)(128)(4,1)S(1)} %get-tuple-element.86, ...), kind=kLoop, calls=%fused_computation.42 | loop fusion | flops 11140864 | bytes 8000512 | tf_op jit(solution)/shard_map/reduce_sum | solution.py:388
  120.1 0.0 slice-start
  120.1 0.0 copy-start.8
  120.1 0.0 slice-start.1
  120.2 2.5 %multiply_reduce_fusion = (f32[256]{0:T(256)S(1)}, bf16[256,2560]{1,0:T(8,128)(2,1)}) fusion(f32[256,2560]{1,0:T(8,128)S(1)} %copy-done.6, f32[256]{0:T(256)S(1)} %get-tuple-element.15, f32[256]{0:T(256)S(1)} %add_divide_fusion.1, f32[256]{0:T(256)S(1)} %get-tuple-element.77, f32[256,2560]{1,0:T(8,128)S(1)} %get-tuple-element.16, ...), kind=kLoop, calls=%fused_computation.41 | loop fusion | flops 10485504 | bytes 10490880 | tf_op jit(solution)/shard_map/reduce_sum | solution.py:391
  122.7 1.5 fusion.16
  124.2 0.0 slice-start.3
  124.2 2.2 %fusion.31 = f32[1280,256]{1,0:T(8,128)S(1)} fusion(bf16[1280,2560]{1,0:T(8,128)(2,1)S(1)} %bitcast.74, bf16[256,2560]{1,0:T(8,128)(2,1)S(1)} %copy-done.8, f32[256,2560]{1,0:T(8,128)S(1)} %get-tuple-element.80, f32[256]{0:T(256)S(1)} %get-tuple-element.9, f32[256]{0:T(256)S(1)} %get-tuple-element.72, f32[256]{0:T(256)S(1)} %get-tuple-element.71, ...), kind=kOutput, calls=%fused_computation.54 | convolution fusion | flops 1683619840 | bytes 11801600 | tf_op jit(solution)/shard_map/dot_general | solution.py:29
  126.4 2.4 %fusion.28 = bf16[1280,256]{1,0:T(8,128)(2,1)S(1)} fusion(f32[1280,256]{1,0:T(8,128)S(1)} %fusion.31, bf16[1280,2560]{1,0:T(8,128)(2,1)S(1)} %bitcast.78, f32[256]{0:T(256)S(1)} %add_divide_fusion.1, bf16[256,2560]{1,0:T(8,128)(2,1)S(1)} %copy-done.10, f32[256,2560]{1,0:T(8,128)S(1)} %get-tuple-element.16, f32[256,2560]{1,0:T(8,128)S(1)} %copy-done.6, ...), kind=kOutput, calls=%fused_computation.49 | convolution fusion | flops 1684930560 | bytes 15077376 | tf_op jit(solution)/shard_map/dot_general | solution.py:29
  128.9 0.7 select_select_fusion.out_grads
  129.6 47.8 %return_grads.1 = bf16[160,9216]{1,0:T(8,128)(2,1)S(1)} custom-call(bf16[16,160,256]{2,1,0:T(8,128)(2,1)S(1)} %select_select_fusion.out_grads, s32[16,1,256]{2,1,0:T(1,128)S(1)} %get-tuple-element.8.wanted), custom_call_target="tpu_custom_call" | custom-call | tf_op jit(solution)/shard_map/return_grads/pallas_call | solution.py:311
  177.5 1.9 %fusion.24 = bf16[256,2560]{1,0:T(8,128)(2,1)} fusion(bf16[256,2560]{1,0:T(8,128)(2,1)S(1)} %copy-done.8, f32[256,2560]{1,0:T(8,128)S(1)} %get-tuple-element.80, f32[256]{0:T(256)S(1)} %get-tuple-element.10, f32[256]{0:T(256)S(1)} %get-tuple-element.84, f32[256]{0:T(256)S(1)} %get-tuple-element.85, f32[256]{0:T(256)S(1)} %subtract_multiply_fusion, ...), kind=kLoop, calls=%fused_computation.35 | loop fusion | flops 5898240 | bytes 5248000 | tf_op jit(solution)/shard_map/convert_element_type | solution.py:407
  179.4 1.6 copy.12
  (31 shorter events, 0.3 us)
Async XLA Ops:
  2.2 1.8 %copy-start = (bf16[9216,160]{0,1:T(8,128)(2,1)S(1)}, bf16[9216,160]{0,1:T(8,128)(2,1)}, u32[]{:S(2)}) copy-start(bf16[9216,160]{0,1:T(8,128)(2,1)} %param.12) | copy-start | bytes 8847364
  4.0 1.0 copy-start.1
  5.0 1.0 copy-start.2
  83.0 6.0 %copy-start.7 = (bf16[256,2560]{1,0:T(8,128)(2,1)S(1)}, bf16[256,2560]{1,0:T(8,128)(2,1)}, u32[]{:S(2)}) copy-start(bf16[256,2560]{1,0:T(8,128)(2,1)} %param.8) | copy-start | bytes 3932164
  89.0 3.1 %copy-start.3 = (bf16[1,16,80,2560]{3,2,1,0:T(8,128)(2,1)}, bf16[1,16,80,2560]{3,2,1,0:T(8,128)(2,1)S(1)}, u32[]{:S(2)}) copy-start(bf16[1,16,80,2560]{3,2,1,0:T(8,128)(2,1)S(1)} %get-tuple-element.19) | copy-start | bytes 19660804
  89.0 4.7 %copy-start.4 = (bf16[1,16,80,2560]{3,2,1,0:T(8,128)(2,1)}, bf16[1,16,80,2560]{3,2,1,0:T(8,128)(2,1)S(1)}, u32[]{:S(2)}) copy-start(bf16[1,16,80,2560]{3,2,1,0:T(8,128)(2,1)S(1)} %get-tuple-element.20) | copy-start | bytes 19660804
  95.6 1.5 copy-start.5
  95.6 5.1 %copy-start.11 = (s32[256,8]{0,1:T(8,128)S(1)}, s32[256,8]{0,1:T(8,128)}, u32[]{:S(2)}) copy-start(s32[256,8]{0,1:T(8,128)} %param.10) | copy-start | bytes 24580
  95.6 5.2 %copy-start.12 = (f32[4,2560]{1,0:T(4,128)S(1)}, f32[4,2560]{1,0:T(4,128)}, u32[]{:S(2)}) copy-start(f32[4,2560]{1,0:T(4,128)} %param.15) | copy-start | bytes 122884
  97.4 1.1 copy-start.9
  98.5 3.7 %collective-permute-start = (bf16[9,2560]{1,0:T(8,128)(2,1)S(1)}, bf16[9,2560]{1,0:T(8,128)(2,1)S(1)}, u32[]{:S(2)}, u32[]{:S(2)}) collective-permute-start(bf16[9,2560]{1,0:T(8,128)(2,1)S(1)} %slice.200), channel_id=1, source_target_pairs={{0,1},{1,2},{2,3},{3,4},{4,5},{5,6},{6,7},{7,8},{8,9},{9,10},{10,1... | collective-permute-start | bytes 138248 | tf_op jit(solution)/shard_map/ppermute | solution.py:21
  102.2 13.9 %copy-start.6 = (f32[256,2560]{1,0:T(8,128)S(1)}, f32[256,2560]{1,0:T(8,128)}, u32[]{:S(2)}) copy-start(f32[256,2560]{1,0:T(8,128)} %copy-done.5) | copy-start | bytes 7864324
  108.8 7.3 %collective-permute-start.1 = (f32[9,2560]{1,0:T(8,128)S(1)}, f32[9,2560]{1,0:T(8,128)S(1)}, u32[]{:S(2)}, u32[]{:S(2)}) collective-permute-start(f32[9,2560]{1,0:T(8,128)S(1)} %slice.205), channel_id=1, source_target_pairs={{1,0},{2,1},{3,2},{4,3},{5,4},{6,5},{7,6},{8,7},{9,8},{10,9},{11,1... | collective-permute-start | bytes 276488 | tf_op jit(solution)/shard_map/ppermute | solution.py:21
  116.1 4.1 %copy-start.10 = (bf16[256,2560]{1,0:T(8,128)(2,1)S(1)}, bf16[256,2560]{1,0:T(8,128)(2,1)}, u32[]{:S(2)}) copy-start(bf16[256,2560]{1,0:T(8,128)(2,1)} %param.9) | copy-start | bytes 3932164
  120.1 4.0 %slice-start = ((s8[6553600]{0:T(1024)(128)(4,1)}), s8[4194304]{0:T(1024)(128)(4,1)S(1)}, s32[]{:S(2)}) async-start(s8[6553600]{0:T(1024)(128)(4,1)} %bitcast.72), calls=%async_computation | async-start | bytes 8388608
  120.1 2.5 %copy-start.8 = (bf16[256,2560]{1,0:T(8,128)(2,1)S(1)}, bf16[256,2560]{1,0:T(8,128)(2,1)}, u32[]{:S(2)}) copy-start(bf16[256,2560]{1,0:T(8,128)(2,1)} %param.8) | copy-start | bytes 3932164
  120.1 4.0 %slice-start.1 = ((s8[6553600]{0:T(1024)(128)(4,1)}), s8[2359296]{0:T(1024)(128)(4,1)S(1)}, s32[]{:S(2)}) async-start(s8[6553600]{0:T(1024)(128)(4,1)} %bitcast.72), calls=%async_computation.1 | async-start | bytes 4718592
  122.7 3.7 %slice-start.2 = ((s8[6553600]{0:T(1024)(128)(4,1)}), s8[4194304]{0:T(1024)(128)(4,1)S(1)}, s32[]{:S(2)}) async-start(s8[6553600]{0:T(1024)(128)(4,1)} %bitcast.76), calls=%async_computation.2 | async-start | bytes 8388608
  124.2 2.2 %slice-start.3 = ((s8[6553600]{0:T(1024)(128)(4,1)}), s8[2359296]{0:T(1024)(128)(4,1)S(1)}, s32[]{:S(2)}) async-start(s8[6553600]{0:T(1024)(128)(4,1)} %bitcast.76), calls=%async_computation.3 | async-start | bytes 4718592
